TPU v7x, 128 devices: a whole 4x4x4 slice. The times are simulated.
128 devices in a mesh: az: 32 (over x, y_hi, z), rad: 4 (over y_lo, core).
Axes of the slice: x: 4, y: 4 (y_hi: 2, y_lo: 2; y = y_hi * 2 + y_lo), z: 4, core: 2. Of those that a mesh axis runs over, the one named last changes fastest.
Arguments:
- state: float32 [8, 128, 32768], P(None, 'rad', 'az'), as said below
- row_shift: int32 [128], replicated, may hold values from 0 to 1023
- row_frac: float32 [128], replicated, may hold values from 0 to 1
- edge_shift: int32 [1], replicated, may hold values from 0 to 1023
- edge_frac: float32 [1], replicated, may hold values from 0 to 1
Outputs:
- new_state: float32 [8, 128, 32768], P(None, 'rad', 'az')
Inputs may be any that keep to these rules, and one draw needn't show every extreme that they name: `state`: field 0 (density) lies between 0.5 and 2 and field 7 (tracer) is positive.
All inputs are finite; a program needn't handle non-finite values.
Results may differ from a plain program's by a relative error of at most 0.00002.
Values sent between devices are 32-bit elements; how exact they have to be, the bound alone decides.
A program may use at most 128 MiB of HBM per device.

v0:
```python
import jax
import jax.numpy as jnp
from jax import lax
from jax.sharding import PartitionSpec as P

NZ = 32


time_step = 0.2
sound_sq = 1.0
rotation = 1.0
shear_rate = 1.5


def passed_along(block, axis, distance):
    devices = range(lax.axis_size(axis))
    route = [((i - distance) % len(devices), i) for i in devices]
    return lax.ppermute(block, axis, route)


def with_halo(cells, sides, width):
    for axis, dim in sides:
        count = lax.axis_size(axis)
        head = lax.slice_in_dim(cells, 0, width, axis=dim)
        tail = lax.slice_in_dim(cells, cells.shape[dim] - width, cells.shape[dim], axis=dim)
        cells = jnp.concatenate(
            [
                lax.ppermute(tail, axis, [(i, (i + 1) % count) for i in range(count)]),
                cells,
                lax.ppermute(head, axis, [((i + 1) % count, i) for i in range(count)]),
            ],
            axis=dim,
        )
    return cells


def plus_x(field):
    return jnp.roll(field, -1, axis=0)


def minus_x(field):
    return jnp.roll(field, 1, axis=0)


def plus_y(field):
    return jnp.roll(field, -NZ, axis=1)


def minus_y(field):
    return jnp.roll(field, NZ, axis=1)


def plus_z(field):
    level = jnp.arange(field.shape[1]) % NZ
    return jnp.where(
        level[None, :] == NZ - 1, jnp.roll(field, NZ - 1, axis=1), jnp.roll(field, -1, axis=1)
    )


def minus_z(field):
    level = jnp.arange(field.shape[1]) % NZ
    return jnp.where(
        level[None, :] == 0, jnp.roll(field, 1 - NZ, axis=1), jnp.roll(field, 1, axis=1)
    )


def side_flux(cells, normal, face_field):
    density, momenta, magnetic, tracer = cells
    velocity = [m / density for m in momenta]
    field_b = list(magnetic)
    field_b[normal] = face_field
    b_square = field_b[0] * field_b[0] + field_b[1] * field_b[1] + field_b[2] * field_b[2]
    pressure = sound_sq * density + 0.5 * b_square
    normal_speed = velocity[normal]
    fluxes = [density * normal_speed]
    for axis_index in range(3):
        flux_term = momenta[axis_index] * normal_speed - face_field * field_b[axis_index]
        if axis_index == normal:
            flux_term = flux_term + pressure
        fluxes.append(flux_term)
    fluxes.append(tracer * normal_speed)
    conserved = [density] + list(momenta) + [tracer]
    signal = jnp.abs(normal_speed) + jnp.sqrt(sound_sq + b_square / density)
    return (fluxes, conserved, signal)


def face_flux(cells, step_back, normal, face_field):
    density, momenta, magnetic, tracer = cells
    behind = (
        step_back(density),
        tuple((step_back(m) for m in momenta)),
        tuple((step_back(b) for b in magnetic)),
        step_back(tracer),
    )
    left_flux, left_cons, left_signal = side_flux(behind, normal, face_field)
    right_flux, right_cons, right_signal = side_flux(cells, normal, face_field)
    bound = jnp.maximum(left_signal, right_signal)
    result = []
    for position in range(5):
        result.append(
            0.5 * (left_flux[position] + right_flux[position])
            - 0.5 * bound * (right_cons[position] - left_cons[position])
        )
    return result


def advance(block):
    density = block[0]
    momenta = (block[1], block[2], block[3])
    faces = (block[4], block[5], block[6])
    tracer = block[7]
    centred = (
        0.5 * (faces[0] + plus_x(faces[0])),
        0.5 * (faces[1] + plus_y(faces[1])),
        0.5 * (faces[2] + plus_z(faces[2])),
    )
    cells = (density, momenta, centred, tracer)
    flux_x = face_flux(cells, minus_x, 0, faces[0])
    flux_y = face_flux(cells, minus_y, 1, faces[1])
    flux_z = face_flux(cells, minus_z, 2, faces[2])
    conserved = [density] + list(momenta) + [tracer]
    updated = []
    for position in range(5):
        change = plus_x(flux_x[position]) - flux_x[position]
        change = change + plus_y(flux_y[position]) - flux_y[position]
        change = change + plus_z(flux_z[position]) - flux_z[position]
        updated.append(conserved[position] - time_step * change)
    updated[1] = updated[1] + time_step * 2.0 * rotation * momenta[1]
    updated[2] = updated[2] - time_step * (2.0 - shear_rate) * rotation * momenta[0]
    velocity = [m / density for m in momenta]
    emf_x = -(velocity[1] * centred[2] - velocity[2] * centred[1])
    emf_y = -(velocity[2] * centred[0] - velocity[0] * centred[2])
    emf_z = -(velocity[0] * centred[1] - velocity[1] * centred[0])
    edge_x = 0.25 * (emf_x + minus_y(emf_x) + minus_z(emf_x) + minus_y(minus_z(emf_x)))
    edge_y = 0.25 * (emf_y + minus_x(emf_y) + minus_z(emf_y) + minus_x(minus_z(emf_y)))
    edge_z = 0.25 * (emf_z + minus_x(emf_z) + minus_y(emf_z) + minus_x(minus_y(emf_z)))
    next_face_x = faces[0] - time_step * (plus_y(edge_z) - edge_z - (plus_z(edge_y) - edge_y))
    next_face_y = faces[1] - time_step * (plus_z(edge_x) - edge_x - (plus_x(edge_z) - edge_z))
    next_face_z = faces[2] - time_step * (plus_x(edge_y) - edge_y - (plus_y(edge_x) - edge_x))
    return jnp.stack(
        [
            updated[0],
            updated[1],
            updated[2],
            updated[3],
            next_face_x,
            next_face_y,
            next_face_z,
            updated[4],
        ]
    )


def slide_rows(joined, steps, largest):
    result = joined
    for position in range(max(1, largest.bit_length())):
        moved = jnp.roll(result, -(1 << position) * NZ, axis=-1)
        chosen = steps // (1 << position) % 2 == 1
        result = jnp.where(chosen[None, :, None], moved, result)
    return result


def window_rows(nearer, farther, remainder, fraction, cells):
    joined = jnp.concatenate([farther, nearer], axis=-1)
    steps = cells - remainder - 1
    length = (cells + 1) * NZ
    window = slide_rows(joined, steps, cells - 1)[..., :length]
    weight = fraction[None, :, None]
    return (1.0 - weight) * window[..., NZ:] + weight * window[..., : cells * NZ]


def loop_blocks(data, quotient, cycle_size):
    carried = data
    for position in range((cycle_size - 1).bit_length()):
        passed = passed_along(carried, "az", 1 << position)
        chosen = quotient // (1 << position) % 2 == 1
        carried = jnp.where(chosen[None, :, None], passed, carried)
    before = passed_along(carried, "az", 1)
    return (carried, before)


def per_device(state, row_shift, row_frac, edge_shift, edge_frac):
    rows = state.shape[1]
    cells = state.shape[2] // NZ
    cycle_size = lax.axis_size("az")
    radial_size = lax.axis_size("rad")
    total = cells * cycle_size
    radial_index = lax.axis_index("rad")
    first_row = radial_index * rows
    local_shift = lax.dynamic_slice_in_dim(row_shift, first_row, rows)
    local_frac = lax.dynamic_slice_in_dim(row_frac, first_row, rows)
    at_inner = radial_index == 0
    at_outer = radial_index == radial_size - 1
    inner_shift = jnp.where(at_inner, edge_shift[0], 0)
    outer_shift = jnp.where(at_outer, total - 1 - edge_shift[0], 0)
    ghost_shift = jnp.stack([inner_shift, inner_shift, outer_shift, outer_shift])
    inner_frac = jnp.where(at_inner, edge_frac[0], 0.0)
    outer_frac = jnp.where(at_outer, 1.0 - edge_frac[0], 0.0)
    ghost_frac = jnp.stack([inner_frac, inner_frac, outer_frac, outer_frac])
    carried, before = loop_blocks(state, local_shift // cells, cycle_size)
    moved = window_rows(carried, before, local_shift % cells, local_frac, cells)
    padded = with_halo(moved, (("rad", 1),), 2)
    ghosts = jnp.concatenate([padded[:, :2], padded[:, -2:]], axis=1)
    ghost_quotient = ghost_shift // cells
    ghost_remainder = ghost_shift % cells
    carried_ghost = ghosts
    for position in range((cycle_size - 1).bit_length()):
        passed_ghost = passed_along(carried_ghost, "az", 1 << position)
        chosen_ghost = ghost_quotient // (1 << position) % 2 == 1
        carried_ghost = jnp.where(chosen_ghost[None, :, None], passed_ghost, carried_ghost)
    before_ghost = passed_along(carried_ghost, "az", 1)
    sheared = window_rows(carried_ghost, before_ghost, ghost_remainder, ghost_frac, cells)
    extended = jnp.concatenate([sheared[:, :2], moved, sheared[:, 2:]], axis=1)
    extended = with_halo(extended, (("az", 2),), 2 * NZ)
    return advance(extended)[:, 2:-2, 2 * NZ : -2 * NZ]


def solution(mesh):
    return jax.shard_map(
        per_device,
        mesh=mesh,
        in_specs=(P(None, "rad", "az"), P(), P(), P(), P()),
        out_specs=P(None, "rad", "az"),
        check_vma=False,
    )
```

profile of v0, /device:TPU:8, one launch (start us, length us, event | category | flops | bytes accessed | tf_op | source)
XLA Modules:
  0.0 260.7 jit_solution(15145326158239422990)
XLA Ops:
  0.0 1.9 collective-permute-start
  1.9 0.8 fusion.116
  2.7 0.8 fusion.121
  3.5 27.9 %collective-permute-done = f32[8,32,1024]{2,1,0:T(8,128)S(1)} collective-permute-done((f32[8,32,1024]{2,1,0:T(8,128)}, f32[8,32,1024]{2,1,0:T(8,128)S(1)}, u32[]{:S(2)}, u32[]{:S(2)}) %collective-permute-start) | collective-permute-done | bytes 1048608 | tf_op jit(solution)/shard_map/ppermute | solution.py:18
  31.3 1.4 broadcast_select_fusion
  32.8 30.3 %collective-permute-done.1 = f32[8,32,1024]{2,1,0:T(8,128)S(1)} collective-permute-done((f32[8,32,1024]{2,1,0:T(8,128)S(1)}, f32[8,32,1024]{2,1,0:T(8,128)S(1)}, u32[]{:S(2)}, u32[]{:S(2)}) %collective-permute-start.1) | collective-permute-done | bytes 1048608 | tf_op jit(solution)/shard_map/ppermute | solution.py:18
  63.5 27.5 %collective-permute-done.2 = f32[8,32,1024]{2,1,0:T(8,128)S(1)} collective-permute-done((f32[8,32,1024]{2,1,0:T(8,128)S(1)}, f32[8,32,1024]{2,1,0:T(8,128)S(1)}, u32[]{:S(2)}, u32[]{:S(2)}) %collective-permute-start.2) | collective-permute-done | bytes 1048608 | tf_op jit(solution)/shard_map/ppermute | solution.py:18
  91.3 23.2 %collective-permute-done.3 = f32[8,32,1024]{2,1,0:T(8,128)S(1)} collective-permute-done((f32[8,32,1024]{2,1,0:T(8,128)S(1)}, f32[8,32,1024]{2,1,0:T(8,128)S(1)}, u32[]{:S(2)}, u32[]{:S(2)}) %collective-permute-start.3) | collective-permute-done | bytes 1048608 | tf_op jit(solution)/shard_map/ppermute | solution.py:18
  114.9 22.6 %collective-permute-done.4 = f32[8,32,1024]{2,1,0:T(8,128)S(1)} collective-permute-done((f32[8,32,1024]{2,1,0:T(8,128)S(1)}, f32[8,32,1024]{2,1,0:T(8,128)S(1)}, u32[]{:S(2)}, u32[]{:S(2)}) %collective-permute-start.4) | collective-permute-done | bytes 1048608 | tf_op jit(solution)/shard_map/ppermute | solution.py:18
  138.7 25.0 %collective-permute-done.5 = f32[8,32,1024]{2,1,0:T(8,128)S(1)} collective-permute-done((f32[8,32,1024]{2,1,0:T(8,128)S(1)}, f32[8,32,1024]{2,1,0:T(8,128)S(1)}, u32[]{:S(2)}, u32[]{:S(2)}) %collective-permute-start.5) | collective-permute-done | bytes 1048608 | tf_op jit(solution)/shard_map/ppermute | solution.py:18
  163.7 0.6 fusion
  164.4 0.4 fusion.1
  164.8 0.6 slice.841
  165.4 0.4 maximum_select_fusion
  166.0 0.4 maximum_select_fusion.1
  166.6 0.4 maximum_select_fusion.2
  167.1 0.3 maximum_select_fusion.3
  167.5 0.4 fusion.2
  168.1 0.5 collective-permute-start.6
  168.6 1.4 collective-permute-done.7
  170.0 2.4 collective-permute-done.6
  172.5 11.0 %collective-permute-done.8 = f32[8,4,1024]{2,1,0:T(4,128)S(1)} collective-permute-done((f32[8,4,1024]{2,1,0:T(4,128)S(1)}, f32[8,4,1024]{2,1,0:T(4,128)S(1)}, u32[]{:S(2)}, u32[]{:S(2)}) %collective-permute-start.8) | collective-permute-done | bytes 131104 | tf_op jit(solution)/shard_map/ppermute | solution.py:18
  183.7 11.5 %collective-permute-done.9 = f32[8,4,1024]{2,1,0:T(4,128)S(1)} collective-permute-done((f32[8,4,1024]{2,1,0:T(4,128)S(1)}, f32[8,4,1024]{2,1,0:T(4,128)S(1)}, u32[]{:S(2)}, u32[]{:S(2)}) %collective-permute-start.9) | collective-permute-done | bytes 131104 | tf_op jit(solution)/shard_map/ppermute | solution.py:18
  195.4 9.2 %collective-permute-done.10 = f32[8,4,1024]{2,1,0:T(4,128)S(1)} collective-permute-done((f32[8,4,1024]{2,1,0:T(4,128)S(1)}, f32[8,4,1024]{2,1,0:T(4,128)S(1)}, u32[]{:S(2)}, u32[]{:S(2)}) %collective-permute-start.10) | collective-permute-done | bytes 131104 | tf_op jit(solution)/shard_map/ppermute | solution.py:18
  204.8 7.6 %collective-permute-done.11 = f32[8,4,1024]{2,1,0:T(4,128)S(1)} collective-permute-done((f32[8,4,1024]{2,1,0:T(4,128)S(1)}, f32[8,4,1024]{2,1,0:T(4,128)S(1)}, u32[]{:S(2)}, u32[]{:S(2)}) %collective-permute-start.11) | collective-permute-done | bytes 131104 | tf_op jit(solution)/shard_map/ppermute | solution.py:18
  212.6 6.5 %collective-permute-done.12 = f32[8,4,1024]{2,1,0:T(4,128)S(1)} collective-permute-done((f32[8,4,1024]{2,1,0:T(4,128)S(1)}, f32[8,4,1024]{2,1,0:T(4,128)S(1)}, u32[]{:S(2)}, u32[]{:S(2)}) %collective-permute-start.12) | collective-permute-done | bytes 131104 | tf_op jit(solution)/shard_map/ppermute | solution.py:18
  220.0 9.9 %collective-permute-done.13 = f32[8,4,1024]{2,1,0:T(4,128)S(1)} collective-permute-done((f32[8,4,1024]{2,1,0:T(4,128)S(1)}, f32[8,4,1024]{2,1,0:T(4,128)S(1)}, u32[]{:S(2)}, u32[]{:S(2)}) %collective-permute-start.13) | collective-permute-done | bytes 131104 | tf_op jit(solution)/shard_map/ppermute | solution.py:18
  231.3 0.2 pad_maximum_fusion.1
  231.7 0.3 collective-permute-start.14
  232.0 7.7 %collective-permute-start.15 = (f32[8,36,64]{2,1,0:T(8,128)S(1)}, f32[8,36,64]{2,1,0:T(8,128)S(1)}, u32[]{:S(2)}, u32[]{:S(2)}) collective-permute-start(f32[8,36,64]{2,1,0:T(8,128)S(1)} %get-tuple-element.94), channel_id=1, source_target_pairs={{4,0},{8,4},{12,8},{16,12},{20,16},{24,20},{28,24},{32,28},{36,32}... | collective-permute-start | bytes 221192 | tf_op jit(solution)/shard_map/ppermute | solution.py:30
  239.7 3.3 %collective-permute-done.14 = f32[8,36,64]{2,1,0:T(8,128)S(1)} collective-permute-done((f32[8,36,64]{2,1,0:T(8,128)S(1)}, f32[8,36,64]{2,1,0:T(8,128)S(1)}, u32[]{:S(2)}, u32[]{:S(2)}) %collective-permute-start.14) | collective-permute-done | bytes 73760 | tf_op jit(solution)/shard_map/ppermute | solution.py:28
  243.0 1.0 concatenate.1380
  246.0 0.5 multiply_subtract_fusion
  246.5 0.3 multiply_subtract_fusion.5
  246.9 0.4 multiply_subtract_fusion.2
  248.1 0.4 multiply_subtract_fusion.1
  248.5 0.3 multiply_subtract_fusion.4
  248.9 0.3 multiply_subtract_fusion.3
  249.6 0.3 multiply_subtract_fusion.8
  250.7 0.3 subtract_negate_fusion
  254.6 1.3 fusion.18
  255.9 0.7 fusion.31
  256.6 0.7 fusion.39
  257.4 0.7 fusion.46
  258.1 0.4 fusion.50
  258.5 0.3 fusion.68
  258.9 0.5 fusion.82
  259.4 1.3 slice.1022
  (186 shorter events, 12.1 us)
Async XLA Ops:
  0.0 31.3 %collective-permute-start = (f32[8,32,1024]{2,1,0:T(8,128)}, f32[8,32,1024]{2,1,0:T(8,128)S(1)}, u32[]{:S(2)}, u32[]{:S(2)}) collective-permute-start(f32[8,32,1024]{2,1,0:T(8,128)} %param.5), channel_id=1, source_target_pairs={{124,0},{0,4},{4,8},{8,12},{12,16},{16,20},{20,24},{24,28},{28,32}... | collective-permute-start | bytes 3145736 | tf_op jit(solution)/shard_map/ppermute | solution.py:18
  32.8 30.4 %collective-permute-start.1 = (f32[8,32,1024]{2,1,0:T(8,128)S(1)}, f32[8,32,1024]{2,1,0:T(8,128)S(1)}, u32[]{:S(2)}, u32[]{:S(2)}) collective-permute-start(f32[8,32,1024]{2,1,0:T(8,128)S(1)} %broadcast_select_fusion), channel_id=1, source_target_pairs={{120,0},{124,4},{0,8},{4,12},{8,16},{12,20},{16,24},{20,28},{24,32... | collective-permute-start | bytes 3145736 | tf_op jit(solution)/shard_map/ppermute | solution.py:18
  63.4 27.6 %collective-permute-start.2 = (f32[8,32,1024]{2,1,0:T(8,128)S(1)}, f32[8,32,1024]{2,1,0:T(8,128)S(1)}, u32[]{:S(2)}, u32[]{:S(2)}) collective-permute-start(f32[8,32,1024]{2,1,0:T(8,128)S(1)} %broadcast_select_fusion.1), channel_id=1, source_target_pairs={{112,0},{116,4},{120,8},{124,12},{0,16},{4,20},{8,24},{12,28},{16,... | collective-permute-start | bytes 3145736 | tf_op jit(solution)/shard_map/ppermute | solution.py:18
  91.3 23.3 %collective-permute-start.3 = (f32[8,32,1024]{2,1,0:T(8,128)S(1)}, f32[8,32,1024]{2,1,0:T(8,128)S(1)}, u32[]{:S(2)}, u32[]{:S(2)}) collective-permute-start(f32[8,32,1024]{2,1,0:T(8,128)S(1)} %broadcast_select_fusion.2), channel_id=1, source_target_pairs={{96,0},{100,4},{104,8},{108,12},{112,16},{116,20},{120,24},{124,28... | collective-permute-start | bytes 3145736 | tf_op jit(solution)/shard_map/ppermute | solution.py:18
  114.8 22.7 %collective-permute-start.4 = (f32[8,32,1024]{2,1,0:T(8,128)S(1)}, f32[8,32,1024]{2,1,0:T(8,128)S(1)}, u32[]{:S(2)}, u32[]{:S(2)}) collective-permute-start(f32[8,32,1024]{2,1,0:T(8,128)S(1)} %broadcast_select_fusion.3), channel_id=1, source_target_pairs={{64,0},{68,4},{72,8},{76,12},{80,16},{84,20},{88,24},{92,28},{96,3... | collective-permute-start | bytes 3145736 | tf_op jit(solution)/shard_map/ppermute | solution.py:18
  137.5 1.0 copy-start
  137.7 26.0 %collective-permute-start.5 = (f32[8,32,1024]{2,1,0:T(8,128)S(1)}, f32[8,32,1024]{2,1,0:T(8,128)S(1)}, u32[]{:S(2)}, u32[]{:S(2)}) collective-permute-start(f32[8,32,1024]{2,1,0:T(8,128)S(1)} %broadcast_select_fusion.4), channel_id=1, source_target_pairs={{124,0},{0,4},{4,8},{8,12},{12,16},{16,20},{20,24},{24,28},{28,32}... | collective-permute-start | bytes 3145736 | tf_op jit(solution)/shard_map/ppermute | solution.py:18
  168.0 2.0 collective-permute-start.7
  168.1 4.3 %collective-permute-start.6 = (f32[8,2,1024]{2,1,0:T(2,128)S(1)}, f32[8,2,1024]{2,1,0:T(2,128)S(1)}, u32[]{:S(2)}, u32[]{:S(2)}) collective-permute-start(f32[8,2,1024]{2,1,0:T(2,128)S(1)} %get-tuple-element.96), channel_id=1, source_target_pairs={{0,1},{1,2},{2,3},{3,0},{4,5},{5,6},{6,7},{7,4},{8,9},{9,10},{10,1... | collective-permute-start | bytes 196616 | tf_op jit(solution)/shard_map/ppermute | solution.py:28
  172.4 11.1 %collective-permute-start.8 = (f32[8,4,1024]{2,1,0:T(4,128)S(1)}, f32[8,4,1024]{2,1,0:T(4,128)S(1)}, u32[]{:S(2)}, u32[]{:S(2)}) collective-permute-start(f32[8,4,1024]{2,1,0:T(4,128)S(1)} %pad_maximum_fusion.32), channel_id=1, source_target_pairs={{124,0},{0,4},{4,8},{8,12},{12,16},{16,20},{20,24},{24,28},{28,32}... | collective-permute-start | bytes 393224 | tf_op jit(solution)/shard_map/ppermute | solution.py:18
  183.6 11.5 %collective-permute-start.9 = (f32[8,4,1024]{2,1,0:T(4,128)S(1)}, f32[8,4,1024]{2,1,0:T(4,128)S(1)}, u32[]{:S(2)}, u32[]{:S(2)}) collective-permute-start(f32[8,4,1024]{2,1,0:T(4,128)S(1)} %broadcast_select_fusion.5), channel_id=1, source_target_pairs={{120,0},{124,4},{0,8},{4,12},{8,16},{12,20},{16,24},{20,28},{24,32... | collective-permute-start | bytes 393224 | tf_op jit(solution)/shard_map/ppermute | solution.py:18
  195.3 9.3 %collective-permute-start.10 = (f32[8,4,1024]{2,1,0:T(4,128)S(1)}, f32[8,4,1024]{2,1,0:T(4,128)S(1)}, u32[]{:S(2)}, u32[]{:S(2)}) collective-permute-start(f32[8,4,1024]{2,1,0:T(4,128)S(1)} %broadcast_select_fusion.6), channel_id=1, source_target_pairs={{112,0},{116,4},{120,8},{124,12},{0,16},{4,20},{8,24},{12,28},{16,... | collective-permute-start | bytes 393224 | tf_op jit(solution)/shard_map/ppermute | solution.py:18
  204.7 7.7 %collective-permute-start.11 = (f32[8,4,1024]{2,1,0:T(4,128)S(1)}, f32[8,4,1024]{2,1,0:T(4,128)S(1)}, u32[]{:S(2)}, u32[]{:S(2)}) collective-permute-start(f32[8,4,1024]{2,1,0:T(4,128)S(1)} %broadcast_select_fusion.7), channel_id=1, source_target_pairs={{96,0},{100,4},{104,8},{108,12},{112,16},{116,20},{120,24},{124,28... | collective-permute-start | bytes 393224 | tf_op jit(solution)/shard_map/ppermute | solution.py:18
  212.5 6.6 %collective-permute-start.12 = (f32[8,4,1024]{2,1,0:T(4,128)S(1)}, f32[8,4,1024]{2,1,0:T(4,128)S(1)}, u32[]{:S(2)}, u32[]{:S(2)}) collective-permute-start(f32[8,4,1024]{2,1,0:T(4,128)S(1)} %broadcast_select_fusion.8), channel_id=1, source_target_pairs={{64,0},{68,4},{72,8},{76,12},{80,16},{84,20},{88,24},{92,28},{96,3... | collective-permute-start | bytes 393224 | tf_op jit(solution)/shard_map/ppermute | solution.py:18
  219.1 10.8 %collective-permute-start.13 = (f32[8,4,1024]{2,1,0:T(4,128)S(1)}, f32[8,4,1024]{2,1,0:T(4,128)S(1)}, u32[]{:S(2)}, u32[]{:S(2)}) collective-permute-start(f32[8,4,1024]{2,1,0:T(4,128)S(1)} %broadcast_select_fusion.9), channel_id=1, source_target_pairs={{124,0},{0,4},{4,8},{8,12},{12,16},{16,20},{20,24},{24,28},{28,32}... | collective-permute-start | bytes 393224 | tf_op jit(solution)/shard_map/ppermute | solution.py:18
  231.7 11.3 %collective-permute-start.14 = (f32[8,36,64]{2,1,0:T(8,128)S(1)}, f32[8,36,64]{2,1,0:T(8,128)S(1)}, u32[]{:S(2)}, u32[]{:S(2)}) collective-permute-start(f32[8,36,64]{2,1,0:T(8,128)S(1)} %get-tuple-element.95), channel_id=1, source_target_pairs={{0,4},{4,8},{8,12},{12,16},{16,20},{20,24},{24,28},{28,32},{32,36}... | collective-permute-start | bytes 221192 | tf_op jit(solution)/shard_map/ppermute | solution.py:28
  232.0 11.0 %collective-permute-start.15 = (f32[8,36,64]{2,1,0:T(8,128)S(1)}, f32[8,36,64]{2,1,0:T(8,128)S(1)}, u32[]{:S(2)}, u32[]{:S(2)}) collective-permute-start(f32[8,36,64]{2,1,0:T(8,128)S(1)} %get-tuple-element.94), channel_id=1, source_target_pairs={{4,0},{8,4},{12,8},{16,12},{20,16},{24,20},{28,24},{32,28},{36,32}... | collective-permute-start | bytes 221192 | tf_op jit(solution)/shard_map/ppermute | solution.py:30
where the time goes:
time: 261 us
  waiting for transfers between devices  219 us (84%)
  other arithmetic  18.1 us (7%)
  starting transfers between devices  11.3 us (4%)
  local copies, waits for them, and re-layouts  9.48 us (4%)
    ppermute x12, waiting for transfers between devices, passed_along(): return lax.ppermute(block, axis, route)  212 us
    ppermute x2, starting transfers between devices, with_halo(): lax.ppermute(head, axis, [((i + 1) % count, i) for i in range(count)])  7.81 us
    ppermute x2, waiting for transfers between devices, with_halo(): lax.ppermute(tail, axis, [(i, (i + 1) % count) for i in range(count)])  5.67 us
  transfers between devices with their start and end apart: 16, of which 15 were waited for; matrix products, arithmetic and copies ran while one was open for 1% of the time, Pallas kernels for 0%

commit v1 on v0

v1 whole, which is shorter than its diff:
```python
import jax
import jax.numpy as jnp
from jax import lax
from jax.experimental import pallas as pl
from jax.experimental.pallas import tpu as pltpu
from jax.sharding import PartitionSpec as P

MESH = pl.DeviceIdType.MESH
NZ = 32
FIELDS = 8
ROWS = 32
COLUMNS = 1024
RING = 32
TILE = 128
TILES = RING * COLUMNS // TILE
SLOTS = ROWS + 3
FLIGHT = 16
TIME_STEP = 0.2


def place():
    az, rad = lax.axis_index("az"), lax.axis_index("rad")
    return az // 8, (az // 4) % 2, az % 4, rad // 2, rad % 2


def holder_of(group, row):
    i = row % 16
    low = (group % 2 + i // 4 + (i // 2) % 2) % 2
    return {"az": 2 * i + low, "rad": (1 - group // 2) * 2 + row // 16}


def exchange_kernel(
    state_ref, shift_ref, frac_ref, edge_shift_ref, edge_frac_ref,
    cells_ref,
    rows_ref, held_ref, moved_ref, ghost_ref,
    out_sem, back_sem, ghost_sem, held_sem, row_sem, halo_sem, face_sem,
):
    x, y_hi, z, y_lo, core = place()
    az, rad = lax.axis_index("az"), lax.axis_index("rad")
    parity = (x + y_hi + z) % 2
    group = (1 - y_lo) * 2 + parity
    row = core * 16 + az // 2
    is_last = row == ROWS - 1
    is_low = row < 2
    is_ghost = jnp.logical_or(is_last, is_low)
    at_edge = jnp.logical_or(
        jnp.logical_and(is_last, group == 3), jnp.logical_and(is_low, group == 0)
    )

    barrier = pltpu.get_barrier_semaphore()

    def greet(d, carry):
        pl.semaphore_signal(barrier, inc=1, device_id={"az": d, "rad": group}, device_id_type=MESH)
        return carry

    lax.fori_loop(0, RING, greet, 0)
    for ghost_group, ghost_row in (((rad + 3) % 4, ROWS - 1), ((rad + 1) % 4, 0), ((rad + 1) % 4, 1)):
        pl.semaphore_signal(
            barrier, inc=1, device_id=holder_of(ghost_group, ghost_row), device_id_type=MESH
        )

    def gather(r, carry):
        for t in range(8):
            first_field = (r // 8) * 64 + t * 8 + r % 8
            rows_ref[r, t] = state_ref[pl.ds(first_field, FIELDS, stride=ROWS * 8), :]
        return carry

    lax.fori_loop(0, ROWS, gather, 0)
    pl.semaphore_wait(barrier, jnp.where(is_ghost, 2 * RING, RING))

    offset_parity = (core + parity) % 2

    def send_out(k, carry):
        half, i = k // 16, k % 16
        dx, dz = i % 4, (i // 4 + i) % 4
        dy = (offset_parity + dx + dz) % 2
        target = ((x + dx) % 4) * 8 + ((y_hi + dy) % 2) * 4 + (z + dz) % 4
        copy = pltpu.make_async_remote_copy(
            src_ref=rows_ref.at[half * 16 + target // 2],
            dst_ref=held_ref.at[pl.ds(az * 8, 8)],
            send_sem=out_sem.at[k % FLIGHT],
            recv_sem=held_sem,
            device_id={"az": target, "rad": (1 - y_lo) * 2 + half},
            device_id_type=MESH,
        )

        @pl.when(k >= FLIGHT)
        def _():
            copy.wait_send()

        copy.start()
        return carry

    lax.fori_loop(0, RING, send_out, 0)
    pltpu.make_async_remote_copy(
        src_ref=held_ref, dst_ref=held_ref, send_sem=out_sem.at[0], recv_sem=held_sem,
        device_id={"az": az, "rad": (rad + 2) % 4}, device_id_type=MESH,
    ).wait_recv()

    lane = lax.broadcasted_iota(jnp.int32, (FIELDS, TILE), 1)

    def held_tile(t):
        return held_ref[t]

    def moved_tile(t):
        return moved_ref[t // 8, t % 8]

    def remap(load, shift, fraction):
        def shifted(t, cells):
            whole, part = cells // 4, (cells % 4) * NZ
            here = (t + 2 * TILES - whole) % TILES
            both = jnp.where(lane < TILE - part, load(here), load((here + TILES - 1) % TILES))
            return pltpu.roll(both, part, 1)

        def tile(t):
            return (1.0 - fraction) * shifted(t, shift) + fraction * shifted(t, shift + 1)

        return tile

    def fill(target_ref, tile, d):
        for j in range(8):
            target_ref[d, j] = tile(8 * d + j)
        after, before = tile((8 * d + 8) % TILES), tile((8 * d + TILES - 1) % TILES)
        target_ref[d, 8] = jnp.where(lane < TILE - NZ, after, before)

    first = remap(held_tile, shift_ref[group * ROWS + row], frac_ref[group * ROWS + row])
    edge_shift, edge_frac = edge_shift_ref[0], edge_frac_ref[0]
    second = remap(
        moved_tile,
        jnp.where(is_last, edge_shift, RING * COLUMNS // NZ - 1 - edge_shift),
        jnp.where(is_last, edge_frac, 1.0 - edge_frac),
    )

    @pl.when(at_edge)
    def _():
        def prepare(d, carry):
            fill(moved_ref, first, d)
            return carry

        lax.fori_loop(0, RING, prepare, 0)

    ghost_group = jnp.where(is_last, (group + 1) % 4, (group + 3) % 4)

    def send_back(k, carry):
        dx, dz, dy = k % 4, (k // 4 + k) % 4, (k // 16 + k) % 2
        d = ((x + dx) % 4) * 8 + ((y_hi + dy) % 2) * 4 + (z + dz) % 4
        slot = k % FLIGHT

        @pl.when(jnp.logical_not(at_edge))
        def _():
            fill(moved_ref, first, d)

        copy = pltpu.make_async_remote_copy(
            src_ref=moved_ref.at[d],
            dst_ref=cells_ref.at[row + 1],
            send_sem=back_sem.at[slot],
            recv_sem=row_sem,
            device_id={"az": d, "rad": group},
            device_id_type=MESH,
        )

        @pl.when(k >= FLIGHT)
        def _():
            copy.wait_send()

        copy.start()

        def ghost_row(source_ref):
            return pltpu.make_async_remote_copy(
                src_ref=source_ref.at[d],
                dst_ref=cells_ref.at[jnp.where(is_last, 0, ROWS + 1)],
                send_sem=ghost_sem.at[slot],
                recv_sem=halo_sem.at[jnp.where(is_last, 0, 1)],
                device_id={"az": d, "rad": ghost_group},
                device_id_type=MESH,
            )

        def ghost_face(source_ref):
            return pltpu.make_async_remote_copy(
                src_ref=source_ref.at[d, :, 4:5],
                dst_ref=cells_ref.at[ROWS + 2, :, 4:5],
                send_sem=ghost_sem.at[slot],
                recv_sem=face_sem,
                device_id={"az": d, "rad": ghost_group},
                device_id_type=MESH,
            )

        @pl.when(jnp.logical_and(is_ghost, at_edge))
        def _():
            fill(ghost_ref, second, d)

        for make, wanted in ((ghost_row, jnp.logical_or(is_last, row == 0)), (ghost_face, row == 1)):
            for source_ref, here in ((ghost_ref, at_edge), (moved_ref, jnp.logical_not(at_edge))):
                @pl.when(jnp.logical_and(wanted, here))
                def _(make=make, source_ref=source_ref):
                    ghost_copy = make(source_ref)

                    @pl.when(k >= FLIGHT)
                    def _():
                        ghost_copy.wait_send()

                    ghost_copy.start()

        return carry

    lax.fori_loop(0, RING, send_back, 0)

    def drain(slot, carry):
        def left(source_ref, sem):
            pltpu.make_async_remote_copy(
                src_ref=source_ref, dst_ref=source_ref, send_sem=sem.at[slot], recv_sem=held_sem,
                device_id={"az": az, "rad": (rad + 2) % 4}, device_id_type=MESH,
            ).wait_send()

        left(rows_ref.at[0], out_sem)
        left(moved_ref.at[0], back_sem)

        @pl.when(jnp.logical_or(is_last, row == 0))
        def _():
            left(moved_ref.at[0], ghost_sem)

        @pl.when(row == 1)
        def _():
            left(moved_ref.at[0, :, 4:5], ghost_sem)

        return carry

    lax.fori_loop(0, FLIGHT, drain, 0)

    def arrived(target_ref, sem):
        pltpu.make_async_remote_copy(
            src_ref=target_ref, dst_ref=target_ref, send_sem=out_sem.at[0], recv_sem=sem,
            device_id={"az": az, "rad": (rad + 2) % 4}, device_id_type=MESH,
        ).wait_recv()

    arrived(cells_ref.at[1 : ROWS + 1], row_sem)
    arrived(cells_ref.at[0], halo_sem.at[0])
    arrived(cells_ref.at[ROWS + 1], halo_sem.at[1])
    arrived(cells_ref.at[ROWS + 2, :, 4:5], face_sem)


def exchange(state, row_shift, row_frac, edge_shift, edge_frac):
    vmem, smem = pl.BlockSpec(memory_space=pltpu.VMEM), pl.BlockSpec(memory_space=pltpu.SMEM)
    dma = pltpu.SemaphoreType.DMA
    return pl.pallas_call(
        exchange_kernel,
        out_shape=jax.ShapeDtypeStruct((SLOTS, 9, FIELDS, TILE), jnp.float32),
        in_specs=[vmem, smem, smem, smem, smem],
        out_specs=vmem,
        scratch_shapes=[
            pltpu.VMEM((ROWS, 8, FIELDS, TILE), jnp.float32),
            pltpu.VMEM((TILES, FIELDS, TILE), jnp.float32),
            pltpu.VMEM((RING, 9, FIELDS, TILE), jnp.float32),
            pltpu.VMEM((RING, 9, FIELDS, TILE), jnp.float32),
            dma((FLIGHT,)), dma((FLIGHT,)), dma((FLIGHT,)),
            dma, dma, dma((2,)), dma,
        ],
        compiler_params=pltpu.CompilerParams(
            collective_id=0, has_side_effects=True, vmem_limit_bytes=24 * 2**20
        ),
        name="exchange",
    )(state, row_shift, row_frac, edge_shift, edge_frac)


def side(cell, normal, face):
    density, momenta, magnetic, tracer, inverse = cell
    field = list(magnetic)
    field[normal] = face
    square = field[0] * field[0] + field[1] * field[1] + field[2] * field[2]
    speed = momenta[normal] * inverse
    flux = [momenta[normal]]
    for n in range(3):
        term = momenta[n] * speed - face * field[n]
        if n == normal:
            term = term + (density + 0.5 * square)
        flux.append(term)
    flux.append(tracer * speed)
    reach = 1.0 + square * inverse
    return flux, jnp.abs(speed) + reach * lax.rsqrt(reach)


def face_flux(before, cell, normal, face):
    left, left_signal = side(before, normal, face)
    right, right_signal = side(cell, normal, face)
    bound = jnp.maximum(left_signal, right_signal)
    left_state = [before[0], *before[1], before[3]]
    right_state = [cell[0], *cell[1], cell[3]]
    return [
        0.5 * ((left[n] + right[n]) - bound * (right_state[n] - left_state[n])) for n in range(5)
    ]


def step_kernel(cells_ref, out_ref, flux_ref, part_ref, emf_ref):
    lane = lax.broadcasted_iota(jnp.int32, (8, TILE), 1)
    level = lane % NZ

    def load(field, row, tile):
        return cells_ref[
            pl.ds(((row + 1) * 9 + tile) * FIELDS + field, 8, stride=9 * FIELDS), :
        ]

    def plus_z(v):
        return jnp.where(level == NZ - 1, pltpu.roll(v, NZ - 1, 1), pltpu.roll(v, TILE - 1, 1))

    def minus_z(v):
        return jnp.where(level == 0, pltpu.roll(v, TILE - NZ + 1, 1), pltpu.roll(v, 1, 1))

    def minus_y(before, v):
        return pltpu.roll(jnp.where(lane >= TILE - NZ, before, v), NZ, 1)

    def plus_y(v, after):
        return pltpu.roll(jnp.where(lane < NZ, after, v), TILE - NZ, 1)

    def read(row, tile, after):
        density = load(0, row, tile)
        momenta = [load(n, row, tile) for n in (1, 2, 3)]
        faces = [load(n, row, tile) for n in (4, 5, 6)]
        tracer = load(7, row, tile)
        centred = [
            0.5 * (faces[0] + load(4, row + 1, tile)),
            0.5 * (faces[1] + plus_y(faces[1], load(5, row, after))),
            0.5 * (faces[2] + plus_z(faces[2])),
        ]
        return (density, momenta, centred, tracer, 1.0 / density), faces

    def block(b, carry):
        row = b * 8

        def first(tile, carry):
            before, after = (tile + 8) % 9, (tile + 1) % 9
            lower, _ = read(row - 1, tile, after)
            cell, faces = read(row, tile, after)
            upper, upper_faces = read(row + 1, tile, after)
            density, momenta, centred, tracer, inverse = cell

            def shifted(field):
                return minus_y(load(field, row, before), load(field, row, tile))

            before_bz = shifted(6)
            behind_density = shifted(0)
            behind = (
                behind_density,
                [shifted(n) for n in (1, 2, 3)],
                [
                    minus_y(0.5 * (load(4, row, before) + load(4, row + 1, before)), centred[0]),
                    None,
                    0.5 * (before_bz + plus_z(before_bz)),
                ],
                shifted(7),
                1.0 / behind_density,
            )
            flux_y = face_flux(behind, cell, 1, faces[1])
            for n in range(5):
                flux_ref[tile, n] = flux_y[n]
            flux_low = face_flux(lower, cell, 0, faces[0])
            flux_high = face_flux(cell, upper, 0, upper_faces[0])
            below = (
                minus_z(density),
                [minus_z(m) for m in momenta],
                [minus_z(centred[0]), minus_z(centred[1]), None],
                minus_z(tracer),
                minus_z(inverse),
            )
            flux_z = face_flux(below, cell, 2, faces[2])
            state = [density, *momenta, tracer]
            for n in range(5):
                change = (flux_high[n] - flux_low[n]) + (plus_z(flux_z[n]) - flux_z[n])
                value = state[n] - TIME_STEP * change
                if n == 1:
                    value = value + TIME_STEP * 2.0 * momenta[1]
                if n == 2:
                    value = value - TIME_STEP * 0.5 * momenta[0]
                part_ref[tile, n] = value

            def velocity(c):
                return [m * c[4] for m in c[1]]

            def emf_y(c, v):
                return v[0] * c[2][2] - v[2] * c[2][0]

            def emf_z(c, v):
                return v[1] * c[2][0] - v[0] * c[2][1]

            v_lower, v, v_upper = velocity(lower), velocity(cell), velocity(upper)
            emf_x = v[2] * centred[1] - v[1] * centred[2]
            y_lower, y_here, y_upper = emf_y(lower, v_lower), emf_y(cell, v), emf_y(upper, v_upper)
            z_lower, z_here, z_upper = emf_z(lower, v_lower), emf_z(cell, v), emf_z(upper, v_upper)
            x_below = minus_z(emf_x)
            y_pair = y_here + y_lower
            y_across = y_upper - y_lower
            part_ref[tile, 5] = faces[0] + 0.25 * TIME_STEP * (plus_z(y_pair) - minus_z(y_pair))
            part_ref[tile, 6] = faces[1]
            part_ref[tile, 7] = faces[2] - 0.25 * TIME_STEP * (y_across + minus_z(y_across))
            emf_ref[tile, 0] = z_here + z_lower
            emf_ref[tile, 1] = (plus_z(emf_x) - x_below) - (z_upper - z_lower)
            emf_ref[tile, 2] = emf_x + x_below
            return carry

        lax.fori_loop(0, 9, first, 0)

        def last(tile, carry):
            before, after = (tile + 8) % 9, tile + 1
            rows, columns = pl.ds(row, 8), pl.ds(pl.multiple_of(tile * TILE, TILE), TILE)
            for n, field in enumerate((0, 1, 2, 3, 7)):
                flux = flux_ref[tile, n]
                out_ref[field, rows, columns] = part_ref[tile, n] - TIME_STEP * (
                    plus_y(flux, flux_ref[after, n]) - flux
                )
            around = [
                (emf_ref[before, n], emf_ref[tile, n], emf_ref[after, n]) for n in range(3)
            ]
            across_z = plus_y(around[0][1], around[0][2]) - minus_y(around[0][0], around[0][1])
            pair = around[1][1] + minus_y(around[1][0], around[1][1])
            across_x = plus_y(around[2][1], around[2][2]) - minus_y(around[2][0], around[2][1])
            out_ref[4, rows, columns] = part_ref[tile, 5] - 0.25 * TIME_STEP * across_z
            out_ref[5, rows, columns] = part_ref[tile, 6] - 0.25 * TIME_STEP * pair
            out_ref[6, rows, columns] = part_ref[tile, 7] + 0.25 * TIME_STEP * across_x
            return carry

        lax.fori_loop(0, 8, last, 0)
        return carry

    lax.fori_loop(0, ROWS // 8, block, 0)


def advance(cells):
    return pl.pallas_call(
        step_kernel,
        out_shape=jax.ShapeDtypeStruct((FIELDS, ROWS, COLUMNS), jnp.float32),
        in_specs=[pl.BlockSpec(memory_space=pltpu.VMEM)],
        out_specs=pl.BlockSpec(memory_space=pltpu.VMEM),
        scratch_shapes=[
            pltpu.VMEM((9, 5, 8, TILE), jnp.float32),
            pltpu.VMEM((9, 8, 8, TILE), jnp.float32),
            pltpu.VMEM((9, 3, 8, TILE), jnp.float32),
        ],
        compiler_params=pltpu.CompilerParams(vmem_limit_bytes=16 * 2**20),
        name="advance",
    )(cells.reshape(SLOTS * 9 * FIELDS, TILE))


def per_device(state, row_shift, row_frac, edge_shift, edge_frac):
    tiles = state.reshape(FIELDS, ROWS // 8, 8, COLUMNS // TILE, TILE).transpose(0, 1, 3, 2, 4)
    tiles = tiles.reshape(FIELDS * ROWS * 8, TILE)
    return advance(exchange(tiles, row_shift, row_frac, edge_shift, edge_frac))


def solution(mesh):
    return jax.shard_map(
        per_device,
        mesh=mesh,
        in_specs=(P(None, "rad", "az"), P(), P(), P(), P()),
        out_specs=P(None, "rad", "az"),
        check_vma=False,
    )
```

time: 261 us -> 79 us (0.30)
  the two profiles are of different devices: /device:TPU:8 before, /device:TPU:2 now
where the time goes in v1:
time: 79 us; the launch traced here: 78.8 us
  Pallas kernels  75 us (95%)
  local copies, waits for them, and re-layouts  2.53 us (3%)
  between operations  1.32 us (2%)
    pallas_call x1, Pallas kernels, exchange(): pl.pallas_call(exchange_kernel, out_shape=jax.ShapeDtypeStruct((SLOTS, 9,...  62 us
    pallas_call x1, Pallas kernels, advance(): pl.pallas_call(step_kernel, out_shape=jax.ShapeDtypeStruct((FIELDS, ROWS,...  13 us
    unnamed x6, local copies, waits for them, and re-layouts  2.53 us

profile of v1, /device:TPU:2, one launch (start us, length us, event | category | flops | bytes accessed | tf_op | source)
XLA Modules:
  0.0 78.8 jit_solution(1650659613447395364)
XLA Ops:
  1.3 0.0 copy-start
  1.3 1.2 %copy-done = f32[8,32,1024]{2,1,0:T(8,128)S(1)} copy-done((f32[8,32,1024]{2,1,0:T(8,128)S(1)}, f32[8,32,1024]{2,1,0:T(8,128)}, u32[]{:S(2)}) %copy-start) | copy-done | bytes 1048600
  2.5 0.0 copy-start.1
  2.5 0.7 copy-done.1
  3.2 0.0 copy-start.2
  3.2 0.7 copy-done.2
  3.8 62.0 %exchange.1 = f32[35,9,8,128]{3,2,1,0:T(8,128)S(1)} custom-call(f32[2048,128]{1,0:T(8,128)S(1)} %bitcast.7, s32[128]{0:T(128)S(1)} %copy-done.1, f32[128]{0:T(128)S(1)} %copy-done.2, s32[1]{0:T(128)S(6)} %copy.6.edge_shift_ref, f32[1]{0:T(128)S(6)} %copy.7.edge_frac_ref), custom_call_target="tpu_custom_call" | custom-call | tf_op jit(solution)/shard_map/exchange/pallas_call | solution.py:245
  65.8 13.0 %advance.1 = f32[8,32,1024]{2,1,0:T(8,128)} custom-call(f32[2520,128]{1,0:T(8,128)S(1)} %bitcast.6), custom_call_target="tpu_custom_call" | custom-call | tf_op jit(solution)/shard_map/advance/pallas_call | solution.py:427
Async XLA Ops:
  1.3 1.2 %copy-start = (f32[8,32,1024]{2,1,0:T(8,128)S(1)}, f32[8,32,1024]{2,1,0:T(8,128)}, u32[]{:S(2)}) copy-start(f32[8,32,1024]{2,1,0:T(8,128)} %param.5) | copy-start | bytes 3145732
  2.5 0.7 copy-start.1
  3.2 0.7 copy-start.2

commit v2 on v1

--- a/solution.py
+++ b/solution.py
@@ -15,6 +15,9 @@
 TILES = RING * COLUMNS // TILE
 SLOTS = ROWS + 3
 FLIGHT = 16
+PAD = 16
+GHOSTS = 17
+GHOST_PAD = 24
 TIME_STEP = 0.2
 
 
@@ -29,44 +32,80 @@
     return {"az": 2 * i + low, "rad": (1 - group // 2) * 2 + row // 16}
 
 
+def ghost_source(n):
+    if n < 8:
+        return ROWS - 1, n, 2 * n
+    if n < 16:
+        return 0, n - 8, 2 * n
+    return 1, 4, 17
+
+
 def exchange_kernel(
+    state_hbm, shift_hbm, frac_hbm, edge_shift_hbm, edge_frac_hbm,
+    cells_ref,
     state_ref, shift_ref, frac_ref, edge_shift_ref, edge_frac_ref,
-    cells_ref,
-    rows_ref, held_ref, moved_ref, ghost_ref,
-    out_sem, back_sem, ghost_sem, held_sem, row_sem, halo_sem, face_sem,
+    rows_ref, strips_ref, held_ref, strip_held_ref, moved_ref, moved_strip_ref, ghosts_ref,
+    in_sem, out_sem, strip_sem, back_sem, ghost_sem, held_sem, strip_held_sem, row_sem, ghosts_sem,
 ):
     x, y_hi, z, y_lo, core = place()
     az, rad = lax.axis_index("az"), lax.axis_index("rad")
     parity = (x + y_hi + z) % 2
     group = (1 - y_lo) * 2 + parity
     row = core * 16 + az // 2
-    is_last = row == ROWS - 1
-    is_low = row < 2
-    is_ghost = jnp.logical_or(is_last, is_low)
-    at_edge = jnp.logical_or(
-        jnp.logical_and(is_last, group == 3), jnp.logical_and(is_low, group == 0)
-    )
+    ghost = jnp.where(row == 17, 16, row // 2)
+    has_ghost = jnp.logical_or(row % 2 == 0, row == 17)
+    from_below = ghost < 8
+    ghost_group = jnp.where(from_below, (group + 3) % 4, (group + 1) % 4)
+
+    loads = [
+        pltpu.make_async_copy(source, target, in_sem.at[n])
+        for n, (source, target) in enumerate(
+            (
+                (state_hbm, state_ref), (shift_hbm, shift_ref), (frac_hbm, frac_ref),
+                (edge_shift_hbm, edge_shift_ref), (edge_frac_hbm, edge_frac_ref),
+            )
+        )
+    ]
+    for load in loads:
+        load.start()
 
     barrier = pltpu.get_barrier_semaphore()
 
-    def greet(d, carry):
-        pl.semaphore_signal(barrier, inc=1, device_id={"az": d, "rad": group}, device_id_type=MESH)
-        return carry
-
-    lax.fori_loop(0, RING, greet, 0)
-    for ghost_group, ghost_row in (((rad + 3) % 4, ROWS - 1), ((rad + 1) % 4, 0), ((rad + 1) % 4, 1)):
-        pl.semaphore_signal(
-            barrier, inc=1, device_id=holder_of(ghost_group, ghost_row), device_id_type=MESH
+    def greet(target_group):
+        def one(d, carry):
+            pl.semaphore_signal(
+                barrier, inc=1, device_id={"az": d, "rad": target_group}, device_id_type=MESH
+            )
+            return carry
+
+        lax.fori_loop(0, RING, one, 0)
+
+    greet(group)
+
+    @pl.when(has_ghost)
+    def _():
+        greet(ghost_group)
+
+    for load in loads:
+        load.wait()
+    for n in range(GHOSTS):
+        r, field, _ = ghost_source(n)
+        strips_ref[n] = state_ref[pl.ds(field * 256 + r // 8 * 64 + r % 8, 8, stride=8), :]
+    pl.semaphore_wait(barrier, RING + GHOSTS)
+
+    def send_strip(n):
+        _, _, taker = ghost_source(n)
+        return pltpu.make_async_remote_copy(
+            src_ref=strips_ref.at[n],
+            dst_ref=strip_held_ref.at[pl.ds(pl.multiple_of(az * 8, 8), 8)],
+            send_sem=strip_sem.at[n],
+            recv_sem=strip_held_sem,
+            device_id=holder_of((rad + (1 if n < 8 else 3)) % 4, taker),
+            device_id_type=MESH,
         )
 
-    def gather(r, carry):
-        for t in range(8):
-            first_field = (r // 8) * 64 + t * 8 + r % 8
-            rows_ref[r, t] = state_ref[pl.ds(first_field, FIELDS, stride=ROWS * 8), :]
-        return carry
-
-    lax.fori_loop(0, ROWS, gather, 0)
-    pl.semaphore_wait(barrier, jnp.where(is_ghost, 2 * RING, RING))
+    for n in range(GHOSTS):
+        send_strip(n).start()
 
     offset_parity = (core + parity) % 2
 
@@ -75,8 +114,13 @@
         dx, dz = i % 4, (i // 4 + i) % 4
         dy = (offset_parity + dx + dz) % 2
         target = ((x + dx) % 4) * 8 + ((y_hi + dy) % 2) * 4 + (z + dz) % 4
+        r = half * 16 + target // 2
+        for t in range(8):
+            rows_ref[r, t] = state_ref[
+                pl.ds((r // 8) * 64 + t * 8 + r % 8, FIELDS, stride=ROWS * 8), :
+            ]
         copy = pltpu.make_async_remote_copy(
-            src_ref=rows_ref.at[half * 16 + target // 2],
+            src_ref=rows_ref.at[r],
             dst_ref=held_ref.at[pl.ds(az * 8, 8)],
             send_sem=out_sem.at[k % FLIGHT],
             recv_sem=held_sem,
@@ -92,64 +136,91 @@
         return carry
 
     lax.fori_loop(0, RING, send_out, 0)
-    pltpu.make_async_remote_copy(
-        src_ref=held_ref, dst_ref=held_ref, send_sem=out_sem.at[0], recv_sem=held_sem,
-        device_id={"az": az, "rad": (rad + 2) % 4}, device_id_type=MESH,
-    ).wait_recv()
+
+    def arrived(target_ref, sem):
+        pltpu.make_async_remote_copy(
+            src_ref=target_ref, dst_ref=target_ref, send_sem=out_sem.at[0], recv_sem=sem,
+            device_id={"az": az, "rad": (rad + 2) % 4}, device_id_type=MESH,
+        ).wait_recv()
+
+    arrived(held_ref.at[:TILES], held_sem)
+    for t in range(PAD):
+        held_ref[TILES + t] = held_ref[t]
+
+    @pl.when(has_ghost)
+    def _():
+        arrived(strip_held_ref.at[:TILES], strip_held_sem)
+        strip_held_ref[TILES:, :] = strip_held_ref[:GHOST_PAD, :]
 
     lane = lax.broadcasted_iota(jnp.int32, (FIELDS, TILE), 1)
 
-    def held_tile(t):
-        return held_ref[t]
-
-    def moved_tile(t):
-        return moved_ref[t // 8, t % 8]
-
-    def remap(load, shift, fraction):
-        def shifted(t, cells):
-            whole, part = cells // 4, (cells % 4) * NZ
-            here = (t + 2 * TILES - whole) % TILES
-            both = jnp.where(lane < TILE - part, load(here), load((here + TILES - 1) % TILES))
-            return pltpu.roll(both, part, 1)
-
-        def tile(t):
-            return (1.0 - fraction) * shifted(t, shift) + fraction * shifted(t, shift + 1)
-
-        return tile
-
-    def fill(target_ref, tile, d):
-        for j in range(8):
-            target_ref[d, j] = tile(8 * d + j)
-        after, before = tile((8 * d + 8) % TILES), tile((8 * d + TILES - 1) % TILES)
-        target_ref[d, 8] = jnp.where(lane < TILE - NZ, after, before)
-
-    first = remap(held_tile, shift_ref[group * ROWS + row], frac_ref[group * ROWS + row])
+    def taps_of(cells, weights):
+        taps = []
+        for n, weight in enumerate(weights):
+            part = ((cells + n) % 4) * NZ
+            halo = (lane + part) % TILE < TILE - NZ
+            taps.append((1 - (cells % 4 + n) // 4, part, lane < TILE - part, halo, weight))
+        return cells // 4, taps
+
+    def first_tile(d, whole):
+        return lax.rem(8 * d + 2 * TILES - 3 - whole, TILES)
+
+    shift, fraction = shift_ref[group * ROWS + row], frac_ref[group * ROWS + row]
+    row_whole, row_taps = taps_of(shift, (1.0 - fraction, fraction))
+
+    def fill(d):
+        base = first_tile(d, row_whole)
+        total = [None] * 9
+        for start, part, here, halo, weight in row_taps:
+            block = held_ref[pl.ds(base + start, 11)]
+            both = [jnp.where(here, block[j + 1], block[j]) for j in range(10)]
+            both = both[1:9] + [jnp.where(halo, both[9], both[0])]
+            for j in range(9):
+                term = weight * pltpu.roll(both[j], part, 1)
+                total[j] = term if total[j] is None else total[j] + term
+        for j in range(9):
+            moved_ref[d, j] = total[j]
+
+    source_row = ghost_group * ROWS + jnp.where(from_below, ROWS - 1, ghost // 16)
+    shift, fraction = shift_ref[source_row], frac_ref[source_row]
     edge_shift, edge_frac = edge_shift_ref[0], edge_frac_ref[0]
-    second = remap(
-        moved_tile,
-        jnp.where(is_last, edge_shift, RING * COLUMNS // NZ - 1 - edge_shift),
-        jnp.where(is_last, edge_frac, 1.0 - edge_frac),
+    at_low, at_high = group == 0, group == 3
+    more = jnp.where(
+        from_below,
+        jnp.where(at_low, edge_shift, 0),
+        jnp.where(at_high, RING * COLUMNS // NZ - 1 - edge_shift, 0),
     )
-
-    @pl.when(at_edge)
-    def _():
-        def prepare(d, carry):
-            fill(moved_ref, first, d)
-            return carry
-
-        lax.fori_loop(0, RING, prepare, 0)
-
-    ghost_group = jnp.where(is_last, (group + 1) % 4, (group + 3) % 4)
+    edge = jnp.where(
+        from_below, jnp.where(at_low, edge_frac, 0.0), jnp.where(at_high, 1.0 - edge_frac, 0.0)
+    )
+    strip_whole, strip_taps = taps_of(
+        lax.rem(shift + more, RING * COLUMNS // NZ),
+        (
+            (1.0 - edge) * (1.0 - fraction),
+            (1.0 - edge) * fraction + edge * (1.0 - fraction),
+            edge * fraction,
+        ),
+    )
+
+    def fill_strip(d):
+        base = first_tile(d, strip_whole)
+        inner = outer = None
+        for start, part, here, halo, weight in strip_taps:
+            at = lambda n: strip_held_ref[pl.ds(base + start + n, 8), :]
+            inside = jnp.where(here, at(2), at(1))
+            outside = jnp.where(halo, jnp.where(here, at(10), at(9)), jnp.where(here, at(1), at(0)))
+            inside = weight * pltpu.roll(inside, part, 1)
+            outside = weight * pltpu.roll(outside, part, 1)
+            inner = inside if inner is None else inner + inside
+            outer = outside if outer is None else outer + outside
+        moved_strip_ref[d, 0:8] = inner
+        moved_strip_ref[d, 8:16] = outer
 
     def send_back(k, carry):
         dx, dz, dy = k % 4, (k // 4 + k) % 4, (k // 16 + k) % 2
         d = ((x + dx) % 4) * 8 + ((y_hi + dy) % 2) * 4 + (z + dz) % 4
         slot = k % FLIGHT
-
-        @pl.when(jnp.logical_not(at_edge))
-        def _():
-            fill(moved_ref, first, d)
-
+        fill(d)
         copy = pltpu.make_async_remote_copy(
             src_ref=moved_ref.at[d],
             dst_ref=cells_ref.at[row + 1],
@@ -165,95 +236,76 @@
 
         copy.start()
 
-        def ghost_row(source_ref):
-            return pltpu.make_async_remote_copy(
-                src_ref=source_ref.at[d],
-                dst_ref=cells_ref.at[jnp.where(is_last, 0, ROWS + 1)],
+        @pl.when(has_ghost)
+        def _():
+            fill_strip(d)
+            strip_copy = pltpu.make_async_remote_copy(
+                src_ref=moved_strip_ref.at[d, :9],
+                dst_ref=ghosts_ref.at[pl.ds(pl.multiple_of(ghost * 16, 16), 9)],
                 send_sem=ghost_sem.at[slot],
-                recv_sem=halo_sem.at[jnp.where(is_last, 0, 1)],
-                device_id={"az": d, "rad": ghost_group},
+                recv_sem=ghosts_sem,
+                device_id={"az": d, "rad": group},
                 device_id_type=MESH,
             )
 
-        def ghost_face(source_ref):
-            return pltpu.make_async_remote_copy(
-                src_ref=source_ref.at[d, :, 4:5],
-                dst_ref=cells_ref.at[ROWS + 2, :, 4:5],
-                send_sem=ghost_sem.at[slot],
-                recv_sem=face_sem,
-                device_id={"az": d, "rad": ghost_group},
-                device_id_type=MESH,
-            )
-
-        @pl.when(jnp.logical_and(is_ghost, at_edge))
+            @pl.when(k >= FLIGHT)
+            def _():
+                strip_copy.wait_send()
+
+            strip_copy.start()
+
+        return carry
+
+    lax.fori_loop(0, RING, send_back, 0)
+
+    def left(source_ref, sem):
+        pltpu.make_async_remote_copy(
+            src_ref=source_ref, dst_ref=source_ref, send_sem=sem, recv_sem=held_sem,
+            device_id={"az": az, "rad": (rad + 2) % 4}, device_id_type=MESH,
+        ).wait_send()
+
+    def drain(slot, carry):
+        left(rows_ref.at[0], out_sem.at[slot])
+        left(moved_ref.at[0], back_sem.at[slot])
+
+        @pl.when(has_ghost)
         def _():
-            fill(ghost_ref, second, d)
-
-        for make, wanted in ((ghost_row, jnp.logical_or(is_last, row == 0)), (ghost_face, row == 1)):
-            for source_ref, here in ((ghost_ref, at_edge), (moved_ref, jnp.logical_not(at_edge))):
-                @pl.when(jnp.logical_and(wanted, here))
-                def _(make=make, source_ref=source_ref):
-                    ghost_copy = make(source_ref)
-
-                    @pl.when(k >= FLIGHT)
-                    def _():
-                        ghost_copy.wait_send()
-
-                    ghost_copy.start()
+            left(moved_strip_ref.at[0, :9], ghost_sem.at[slot])
 
         return carry
 
-    lax.fori_loop(0, RING, send_back, 0)
-
-    def drain(slot, carry):
-        def left(source_ref, sem):
-            pltpu.make_async_remote_copy(
-                src_ref=source_ref, dst_ref=source_ref, send_sem=sem.at[slot], recv_sem=held_sem,
-                device_id={"az": az, "rad": (rad + 2) % 4}, device_id_type=MESH,
-            ).wait_send()
-
-        left(rows_ref.at[0], out_sem)
-        left(moved_ref.at[0], back_sem)
-
-        @pl.when(jnp.logical_or(is_last, row == 0))
-        def _():
-            left(moved_ref.at[0], ghost_sem)
-
-        @pl.when(row == 1)
-        def _():
-            left(moved_ref.at[0, :, 4:5], ghost_sem)
-
-        return carry
-
     lax.fori_loop(0, FLIGHT, drain, 0)
-
-    def arrived(target_ref, sem):
-        pltpu.make_async_remote_copy(
-            src_ref=target_ref, dst_ref=target_ref, send_sem=out_sem.at[0], recv_sem=sem,
-            device_id={"az": az, "rad": (rad + 2) % 4}, device_id_type=MESH,
-        ).wait_recv()
+    for n in range(GHOSTS):
+        send_strip(n).wait_send()
 
     arrived(cells_ref.at[1 : ROWS + 1], row_sem)
-    arrived(cells_ref.at[0], halo_sem.at[0])
-    arrived(cells_ref.at[ROWS + 1], halo_sem.at[1])
-    arrived(cells_ref.at[ROWS + 2, :, 4:5], face_sem)
+    arrived(moved_strip_ref.at[:GHOSTS, :9], ghosts_sem)
+    for t in range(9):
+        cells_ref[0, t] = ghosts_ref[pl.ds(t, FIELDS, stride=16), :]
+        cells_ref[ROWS + 1, t] = ghosts_ref[pl.ds(FIELDS * 16 + t, FIELDS, stride=16), :]
+        cells_ref[ROWS + 2, t] = jnp.broadcast_to(ghosts_ref[pl.ds(256 + t, 1), :], (8, TILE))
 
 
 def exchange(state, row_shift, row_frac, edge_shift, edge_frac):
-    vmem, smem = pl.BlockSpec(memory_space=pltpu.VMEM), pl.BlockSpec(memory_space=pltpu.SMEM)
-    dma = pltpu.SemaphoreType.DMA
+    dma, smem = pltpu.SemaphoreType.DMA, pltpu.SMEM
     return pl.pallas_call(
         exchange_kernel,
         out_shape=jax.ShapeDtypeStruct((SLOTS, 9, FIELDS, TILE), jnp.float32),
-        in_specs=[vmem, smem, smem, smem, smem],
-        out_specs=vmem,
+        in_specs=[pl.BlockSpec(memory_space=pltpu.HBM)] * 5,
+        out_specs=pl.BlockSpec(memory_space=pltpu.VMEM),
         scratch_shapes=[
+            pltpu.VMEM(state.shape, jnp.float32),
+            smem(row_shift.shape, jnp.int32), smem(row_frac.shape, jnp.float32),
+            smem((1,), jnp.int32), smem((1,), jnp.float32),
             pltpu.VMEM((ROWS, 8, FIELDS, TILE), jnp.float32),
-            pltpu.VMEM((TILES, FIELDS, TILE), jnp.float32),
+            pltpu.VMEM((GHOSTS, 8, TILE), jnp.float32),
+            pltpu.VMEM((TILES + PAD, FIELDS, TILE), jnp.float32),
+            pltpu.VMEM((TILES + GHOST_PAD, TILE), jnp.float32),
             pltpu.VMEM((RING, 9, FIELDS, TILE), jnp.float32),
-            pltpu.VMEM((RING, 9, FIELDS, TILE), jnp.float32),
-            dma((FLIGHT,)), dma((FLIGHT,)), dma((FLIGHT,)),
-            dma, dma, dma((2,)), dma,
+            pltpu.VMEM((RING, 16, TILE), jnp.float32),
+            pltpu.VMEM((GHOSTS * 16, TILE), jnp.float32),
+            dma((5,)), dma((FLIGHT,)), dma((GHOSTS,)), dma((FLIGHT,)), dma((FLIGHT,)),
+            dma, dma, dma, dma,
         ],
         compiler_params=pltpu.CompilerParams(
             collective_id=0, has_side_effects=True, vmem_limit_bytes=24 * 2**20
@@ -293,6 +345,8 @@
 def step_kernel(cells_ref, out_ref, flux_ref, part_ref, emf_ref):
     lane = lax.broadcasted_iota(jnp.int32, (8, TILE), 1)
     level = lane % NZ
+    up = jnp.where(level == NZ - 1, lane - (NZ - 1), lane + 1)
+    down = jnp.where(level == 0, lane + (NZ - 1), lane - 1)
 
     def load(field, row, tile):
         return cells_ref[
@@ -300,10 +354,10 @@
         ]
 
     def plus_z(v):
-        return jnp.where(level == NZ - 1, pltpu.roll(v, NZ - 1, 1), pltpu.roll(v, TILE - 1, 1))
+        return jnp.take_along_axis(v, up, axis=1, mode="promise_in_bounds")
 
     def minus_z(v):
-        return jnp.where(level == 0, pltpu.roll(v, TILE - NZ + 1, 1), pltpu.roll(v, 1, 1))
+        return jnp.take_along_axis(v, down, axis=1, mode="promise_in_bounds")
 
     def minus_y(before, v):
         return pltpu.roll(jnp.where(lane >= TILE - NZ, before, v), NZ, 1)
@@ -396,7 +450,7 @@
             emf_ref[tile, 2] = emf_x + x_below
             return carry
 
-        lax.fori_loop(0, 9, first, 0)
+        lax.fori_loop(0, 9, first, 0, unroll=9)
 
         def last(tile, carry):
             before, after = (tile + 8) % 9, tile + 1
@@ -417,7 +471,7 @@
             out_ref[6, rows, columns] = part_ref[tile, 7] + 0.25 * TIME_STEP * across_x
             return carry
 
-        lax.fori_loop(0, 8, last, 0)
+        lax.fori_loop(0, 8, last, 0, unroll=8)
         return carry
 
     lax.fori_loop(0, ROWS // 8, block, 0)

time: 79 us -> 53.2 us (0.67)
  the two profiles are of different devices: /device:TPU:2 before, /device:TPU:34 now
where the time goes in v2:
time: 53.2 us; the launch traced here: 53 us
  Pallas kernels  49.1 us (92%)
  local copies, waits for them, and re-layouts  2.53 us (5%)
  between operations  1.32 us (2%)
    pallas_call x1, Pallas kernels, exchange(): pl.pallas_call(exchange_kernel, out_shape=jax.ShapeDtypeStruct((SLOTS, 9,...  43.7 us
    pallas_call x1, Pallas kernels, advance(): pl.pallas_call(step_kernel, out_shape=jax.ShapeDtypeStruct((FIELDS, ROWS,...  5.41 us
    unnamed x6, local copies, waits for them, and re-layouts  2.53 us

profile of v2, /device:TPU:34, one launch (start us, length us, event | category | flops | bytes accessed | tf_op | source)
XLA Modules:
  0.0 53.0 jit_solution(12234790078278171073)
XLA Ops:
  1.3 0.0 copy-start
  1.3 1.2 %copy-done = f32[8,32,1024]{2,1,0:T(8,128)S(1)} copy-done((f32[8,32,1024]{2,1,0:T(8,128)S(1)}, f32[8,32,1024]{2,1,0:T(8,128)}, u32[]{:S(2)}) %copy-start) | copy-done | bytes 1048600
  2.5 0.0 copy-start.1
  2.5 0.7 %copy-done.1 = s32[128]{0:T(128)S(1)} copy-done((s32[128]{0:T(128)S(1)}, s32[128]{0:T(128)}, u32[]{:S(2)}) %copy-start.1) | copy-done | bytes 536
  3.2 0.0 copy-start.2
  3.2 0.7 %copy-done.2 = f32[128]{0:T(128)S(1)} copy-done((f32[128]{0:T(128)S(1)}, f32[128]{0:T(128)}, u32[]{:S(2)}) %copy-start.2) | copy-done | bytes 536
  3.8 43.7 %exchange.1 = f32[35,9,8,128]{3,2,1,0:T(8,128)S(1)} custom-call(f32[2048,128]{1,0:T(8,128)S(1)} %bitcast.7, s32[128]{0:T(128)S(1)} %copy-done.1, f32[128]{0:T(128)S(1)} %copy-done.2, s32[1]{0:T(128)S(6)} %copy.6.edge_shift_hbm, f32[1]{0:T(128)S(6)} %copy.7.edge_frac_hbm), custom_call_target="tpu_custom_call" | custom-call | tf_op jit(solution)/shard_map/exchange/pallas_call | solution.py:291
  47.6 5.4 %advance.1 = f32[8,32,1024]{2,1,0:T(8,128)} custom-call(f32[2520,128]{1,0:T(8,128)S(1)} %bitcast.6), custom_call_target="tpu_custom_call" | custom-call | tf_op jit(solution)/shard_map/advance/pallas_call | solution.py:481
Async XLA Ops:
  1.3 1.2 %copy-start = (f32[8,32,1024]{2,1,0:T(8,128)S(1)}, f32[8,32,1024]{2,1,0:T(8,128)}, u32[]{:S(2)}) copy-start(f32[8,32,1024]{2,1,0:T(8,128)} %param.5) | copy-start | bytes 3145732
  2.5 0.7 %copy-start.1 = (s32[128]{0:T(128)S(1)}, s32[128]{0:T(128)}, u32[]{:S(2)}) copy-start(s32[128]{0:T(128)} %shift_hbm.1) | copy-start | bytes 1540
  3.2 0.7 %copy-start.2 = (f32[128]{0:T(128)S(1)}, f32[128]{0:T(128)}, u32[]{:S(2)}) copy-start(f32[128]{0:T(128)} %frac_hbm.1) | copy-start | bytes 1540

commit v3 on v2

v3 whole, which is shorter than its diff:
```python
import jax
import jax.numpy as jnp
from jax import lax
from jax.experimental import pallas as pl
from jax.experimental.pallas import tpu as pltpu
from jax.sharding import PartitionSpec as P

MESH = pl.DeviceIdType.MESH
NZ = 32
FIELDS = 8
HELD = 4
ROWS = 32
HALF = 16
COLUMNS = 1024
RING = 32
TILE = 128
TILES = RING * COLUMNS // TILE
PAD = 24
WINDOW = 36
LINES = 40
SLOTS = ROWS + 3
GHOSTS = 17
VMEM_LIMIT = 60 * 2**20
TIME_STEP = 0.2


def place():
    az, rad = lax.axis_index("az"), lax.axis_index("rad")
    return az // 8, (az // 4) % 2, az % 4, rad // 2, rad % 2


def holder_of(group, index):
    i = index % 16
    low = (group % 2 + i // 4 + (i // 2) % 2) % 2
    return {"az": 2 * i + low, "rad": (1 - group // 2) * 2 + index // 16}


def ghost_source(n):
    if n < 8:
        return ROWS - 1, n, 2 * n
    if n < 16:
        return 0, n - 8, 2 * n
    return 1, 4, 17


def kernel(
    state_hbm, shift_hbm, frac_hbm, edge_shift_hbm, edge_frac_hbm,
    out_hbm,
    state_ref, shift_ref, frac_ref, edge_shift_ref, edge_frac_ref,
    rows_ref, strips_ref, held_low_ref, held_high_ref, strip_held_ref, moved_ref, moved_strip_ref, cells_ref, ghosts_ref,
    out_ref, flux_ref, part_ref, emf_ref,
    in_sem, rows_sem, strips_sem, back_sem, ghosts_back_sem, held_sem, strip_held_sem, row_sem, ghosts_sem, done_sem,
):
    x, y_hi, z, y_lo, core = place()
    az, rad = lax.axis_index("az"), lax.axis_index("rad")
    parity = (x + y_hi + z) % 2
    group = (1 - y_lo) * 2 + parity
    index = core * 16 + az // 2
    ghost = jnp.where(index == 17, 16, index // 2)
    has_ghost = jnp.logical_or(index % 2 == 0, index == 17)
    from_below = ghost < 8
    ghost_group = jnp.where(from_below, (group + 3) % 4, (group + 1) % 4)

    loads = [
        pltpu.make_async_copy(source, target, in_sem.at[n])
        for n, (source, target) in enumerate(
            (
                (state_hbm, state_ref), (shift_hbm, shift_ref), (frac_hbm, frac_ref),
                (edge_shift_hbm, edge_shift_ref), (edge_frac_hbm, edge_frac_ref),
            )
        )
    ]
    for load in loads:
        load.start()

    barrier = pltpu.get_barrier_semaphore()

    def greet(target_group):
        def one(d, carry):
            pl.semaphore_signal(
                barrier, inc=1, device_id={"az": d, "rad": target_group}, device_id_type=MESH
            )
            return carry

        lax.fori_loop(0, RING, one, 0)

    greet(group)

    @pl.when(has_ghost)
    def _():
        greet(ghost_group)

    for load in loads:
        load.wait()

    def field_lines(field, r):
        return state_ref[pl.ds(field * 256 + r // 8 * 64 + r % 8, 8, stride=8), :]

    for n in range(GHOSTS):
        r, field, _ = ghost_source(n)
        strips_ref[n] = field_lines(field, r)
    pl.semaphore_wait(barrier, RING + GHOSTS)

    for n in range(GHOSTS):
        pltpu.make_async_remote_copy(
            src_ref=strips_ref.at[n],
            dst_ref=strip_held_ref.at[pl.ds(pl.multiple_of(az * 8, 8), 8)],
            send_sem=strips_sem,
            recv_sem=strip_held_sem,
            device_id=holder_of((rad + (1 if n < 8 else 3)) % 4, ghost_source(n)[2]),
            device_id_type=MESH,
        ).start()

    offset_parity = (core + parity) % 2
    held_refs = (held_low_ref, held_high_ref)

    def send_out(half):
        def one(k, carry):
            part, i = k // 16, k % 16
            dx, dz = i % 4, (i // 4 + i) % 4
            dy = (offset_parity + dx + dz) % 2
            target = ((x + dx) % 4) * 8 + ((y_hi + dy) % 2) * 4 + (z + dz) % 4
            r = half * HALF + target // 2
            for f in range(HELD):
                rows_ref[r, part, f] = field_lines(part * HELD + f, r)
            pltpu.make_async_remote_copy(
                src_ref=rows_ref.at[r, part],
                dst_ref=held_refs[half].at[:, pl.ds(pl.multiple_of(az * 8, 8), 8)],
                send_sem=rows_sem,
                recv_sem=held_sem.at[half],
                device_id={"az": target, "rad": (1 - y_lo) * 2 + part},
                device_id_type=MESH,
            ).start()
            return carry

        lax.fori_loop(0, RING, one, 0)

    send_out(0)
    send_out(1)

    def same_size(ref, send_sem, recv_sem):
        return pltpu.make_async_remote_copy(
            src_ref=ref, dst_ref=ref, send_sem=send_sem, recv_sem=recv_sem,
            device_id={"az": az, "rad": (rad + 2) % 4}, device_id_type=MESH,
        )

    lane = lax.broadcasted_iota(jnp.int32, (8, TILE), 1)

    def taps_of(cells, weights):
        taps = []
        for n, weight in enumerate(weights):
            part = ((cells + n) % 4) * NZ
            halo = (lane + part) % TILE < TILE - NZ
            taps.append((1 - (cells % 4 + n) // 4, part, lane < TILE - part, halo, weight))
        return cells // 4, taps

    def blend(taps, tile_lines, halo_lines, fields):
        inner, outer = [None] * fields, None
        for start, part, here, halo, weight in taps:
            for f in range(fields):
                both = jnp.where(here, tile_lines(f, start + 2), tile_lines(f, start + 1))
                term = weight * pltpu.roll(both, part, 1)
                inner[f] = term if inner[f] is None else inner[f] + term
            after = jnp.where(here, halo_lines(start + 10), halo_lines(start + 9))
            before = jnp.where(here, halo_lines(start + 1), halo_lines(start))
            term = weight * pltpu.roll(jnp.where(halo, after, before), part, 1)
            outer = term if outer is None else outer + term
        return inner, outer

    def send_back(half):
        held_ref = held_refs[half]
        same_size(held_ref.at[:, :TILES], rows_sem, held_sem.at[half]).wait_recv()
        for f in range(HELD):
            held_ref[f, TILES:] = held_ref[f, :PAD]
        r = half * HALF + az // 2
        shift, fraction = shift_ref[group * ROWS + r], frac_ref[group * ROWS + r]
        whole, taps = taps_of(shift, (1.0 - fraction, fraction))

        def fill(d):
            base = lax.rem(8 * d + 2 * TILES - 3 - whole, TILES)
            inner, outer = blend(
                taps,
                lambda f, n: held_ref[f, pl.ds(base + n, 8), :],
                lambda n: jnp.concatenate(
                    [held_ref[f, pl.ds(base + n, 1), :] for f in range(HELD)] * 2, axis=0
                ),
                HELD,
            )
            for f in range(HELD):
                moved_ref[half, d, f * 8 : f * 8 + 8] = inner[f]
            moved_ref[half, d, 32:LINES] = outer

        if half == 0:
            strip_whole, strip_taps = ghost_taps()

        def fill_strip(d):
            base = lax.rem(8 * d + 2 * TILES - 3 - strip_whole, TILES)
            lines = lambda n: strip_held_ref[pl.ds(base + n, 8), :]
            inner, outer = blend(strip_taps, lambda f, n: lines(n), lines, 1)
            moved_strip_ref[d, 0:8] = inner[0]
            moved_strip_ref[d, 8:16] = outer

        def one(k, carry):
            dx, dz, dy = k % 4, (k // 4 + k) % 4, (k // 16 + k) % 2
            d = ((x + dx) % 4) * 8 + ((y_hi + dy) % 2) * 4 + (z + dz) % 4
            fill(d)
            pltpu.make_async_remote_copy(
                src_ref=moved_ref.at[half, d, :WINDOW],
                dst_ref=cells_ref.at[pl.ds(pl.multiple_of(((r + 1) * 2 + core) * LINES, 8), WINDOW)],
                send_sem=back_sem,
                recv_sem=row_sem.at[half],
                device_id={"az": d, "rad": group},
                device_id_type=MESH,
            ).start()

            if half == 0:
                @pl.when(has_ghost)
                def _():
                    fill_strip(d)
                    pltpu.make_async_remote_copy(
                        src_ref=moved_strip_ref.at[d, :9],
                        dst_ref=ghosts_ref.at[pl.ds(pl.multiple_of(ghost * 16, 16), 9)],
                        send_sem=ghosts_back_sem,
                        recv_sem=ghosts_sem,
                        device_id={"az": d, "rad": group},
                        device_id_type=MESH,
                    ).start()

            return carry

        lax.fori_loop(0, RING, one, 0)

    def ghost_taps():
        @pl.when(has_ghost)
        def _():
            same_size(strip_held_ref.at[:TILES], strips_sem, strip_held_sem).wait_recv()
            strip_held_ref[TILES:, :] = strip_held_ref[:PAD, :]

        source_row = ghost_group * ROWS + jnp.where(from_below, ROWS - 1, ghost // 16)
        shift, fraction = shift_ref[source_row], frac_ref[source_row]
        edge_shift, edge_frac = edge_shift_ref[0], edge_frac_ref[0]
        at_low, at_high = group == 0, group == 3
        more = jnp.where(
            from_below,
            jnp.where(at_low, edge_shift, 0),
            jnp.where(at_high, RING * COLUMNS // NZ - 1 - edge_shift, 0),
        )
        edge = jnp.where(
            from_below, jnp.where(at_low, edge_frac, 0.0), jnp.where(at_high, 1.0 - edge_frac, 0.0)
        )
        return taps_of(
            lax.rem(shift + more, RING * COLUMNS // NZ),
            (
                (1.0 - edge) * (1.0 - fraction),
                (1.0 - edge) * fraction + edge * (1.0 - fraction),
                edge * fraction,
            ),
        )

    send_back(0)
    send_back(1)

    def finish(block):
        return pltpu.make_async_copy(
            out_ref.at[:, pl.ds(pl.multiple_of(block * 8, 8), 8)],
            out_hbm.at[:, pl.ds(pl.multiple_of(block * 8, 8), 8)],
            done_sem,
        )

    def arrived(half):
        same_size(cells_ref.at[: HALF * 2 * WINDOW], back_sem, row_sem.at[half]).wait_recv()

    arrived(0)
    same_size(ghosts_ref.at[: GHOSTS * 9], ghosts_back_sem, ghosts_sem).wait_recv()
    for n in range(GHOSTS):
        slot, field = ((0, n) if n < 8 else (ROWS + 1, n - 8) if n < 16 else (ROWS + 2, 4))
        first = (slot * 2 + field // HELD) * LINES
        at = first + field % HELD * 8
        cells_ref[at : at + 8] = ghosts_ref[n * 16 : n * 16 + 8]
        cells_ref[first + 32 + field % HELD : first + 33 + field % HELD] = ghosts_ref[n * 16 + 8 : n * 16 + 9]
    step_block(cells_ref, out_ref, flux_ref, part_ref, emf_ref, 0)
    finish(0).start()
    arrived(1)

    def later(block, carry):
        step_block(cells_ref, out_ref, flux_ref, part_ref, emf_ref, block)
        finish(block).start()
        return carry

    lax.fori_loop(1, ROWS // 8, later, 0)

    same_size(rows_ref, rows_sem, held_sem.at[0]).wait_send()
    same_size(strips_ref, strips_sem, held_sem.at[0]).wait_send()
    same_size(moved_ref.at[:, :, :WINDOW], back_sem, held_sem.at[0]).wait_send()

    @pl.when(has_ghost)
    def _():
        same_size(moved_strip_ref.at[:, :9], ghosts_back_sem, held_sem.at[0]).wait_send()

    pltpu.make_async_copy(out_ref, out_hbm, done_sem).wait()


def side(cell, normal, face):
    density, momenta, magnetic, tracer, inverse = cell
    field = list(magnetic)
    field[normal] = face
    square = field[0] * field[0] + field[1] * field[1] + field[2] * field[2]
    speed = momenta[normal] * inverse
    flux = [momenta[normal]]
    for n in range(3):
        term = momenta[n] * speed - face * field[n]
        if n == normal:
            term = term + (density + 0.5 * square)
        flux.append(term)
    flux.append(tracer * speed)
    reach = 1.0 + square * inverse
    return flux, jnp.abs(speed) + reach * lax.rsqrt(reach)


def face_flux(before, cell, normal, face):
    left, left_signal = side(before, normal, face)
    right, right_signal = side(cell, normal, face)
    bound = jnp.maximum(left_signal, right_signal)
    left_state = [before[0], *before[1], before[3]]
    right_state = [cell[0], *cell[1], cell[3]]
    return [
        0.5 * ((left[n] + right[n]) - bound * (right_state[n] - left_state[n])) for n in range(5)
    ]


def step_block(cells_ref, out_ref, flux_ref, part_ref, emf_ref, block):
    lane = lax.broadcasted_iota(jnp.int32, (8, TILE), 1)
    level = lane % NZ
    up = jnp.where(level == NZ - 1, lane - (NZ - 1), lane + 1)
    down = jnp.where(level == 0, lane + (NZ - 1), lane - 1)

    def load(field, row, tile):
        line = field % HELD * 8 + tile if tile < 8 else 32 + field % HELD
        first = ((row + 1) * 2 + field // HELD) * LINES + line
        return cells_ref[pl.ds(first, 8, stride=2 * LINES), :]

    def plus_z(v):
        return jnp.take_along_axis(v, up, axis=1, mode="promise_in_bounds")

    def minus_z(v):
        return jnp.take_along_axis(v, down, axis=1, mode="promise_in_bounds")

    def minus_y(before, v):
        return pltpu.roll(jnp.where(lane >= TILE - NZ, before, v), NZ, 1)

    def plus_y(v, after):
        return pltpu.roll(jnp.where(lane < NZ, after, v), TILE - NZ, 1)

    def read(row, tile, after):
        density = load(0, row, tile)
        momenta = [load(n, row, tile) for n in (1, 2, 3)]
        faces = [load(n, row, tile) for n in (4, 5, 6)]
        tracer = load(7, row, tile)
        centred = [
            0.5 * (faces[0] + load(4, row + 1, tile)),
            0.5 * (faces[1] + plus_y(faces[1], load(5, row, after))),
            0.5 * (faces[2] + plus_z(faces[2])),
        ]
        return (density, momenta, centred, tracer, 1.0 / density), faces

    row = pl.multiple_of(block * 8, 8)

    def first(tile):
        before, after = (tile + 8) % 9, (tile + 1) % 9
        lower, _ = read(row - 1, tile, after)
        cell, faces = read(row, tile, after)
        upper, upper_faces = read(row + 1, tile, after)
        density, momenta, centred, tracer, inverse = cell

        def shifted(field):
            return minus_y(load(field, row, before), load(field, row, tile))

        before_bz = shifted(6)
        behind_density = shifted(0)
        behind = (
            behind_density,
            [shifted(n) for n in (1, 2, 3)],
            [
                minus_y(0.5 * (load(4, row, before) + load(4, row + 1, before)), centred[0]),
                None,
                0.5 * (before_bz + plus_z(before_bz)),
            ],
            shifted(7),
            1.0 / behind_density,
        )
        flux_y = face_flux(behind, cell, 1, faces[1])
        for n in range(5):
            flux_ref[tile, n] = flux_y[n]
        flux_low = face_flux(lower, cell, 0, faces[0])
        flux_high = face_flux(cell, upper, 0, upper_faces[0])
        below = (
            minus_z(density),
            [minus_z(m) for m in momenta],
            [minus_z(centred[0]), minus_z(centred[1]), None],
            minus_z(tracer),
            minus_z(inverse),
        )
        flux_z = face_flux(below, cell, 2, faces[2])
        state = [density, *momenta, tracer]
        for n in range(5):
            change = (flux_high[n] - flux_low[n]) + (plus_z(flux_z[n]) - flux_z[n])
            value = state[n] - TIME_STEP * change
            if n == 1:
                value = value + TIME_STEP * 2.0 * momenta[1]
            if n == 2:
                value = value - TIME_STEP * 0.5 * momenta[0]
            part_ref[tile, n] = value

        def velocity(c):
            return [m * c[4] for m in c[1]]

        def emf_y(c, v):
            return v[0] * c[2][2] - v[2] * c[2][0]

        def emf_z(c, v):
            return v[1] * c[2][0] - v[0] * c[2][1]

        v_lower, v, v_upper = velocity(lower), velocity(cell), velocity(upper)
        emf_x = v[2] * centred[1] - v[1] * centred[2]
        y_lower, y_here, y_upper = emf_y(lower, v_lower), emf_y(cell, v), emf_y(upper, v_upper)
        z_lower, z_here, z_upper = emf_z(lower, v_lower), emf_z(cell, v), emf_z(upper, v_upper)
        x_below = minus_z(emf_x)
        y_pair = y_here + y_lower
        y_across = y_upper - y_lower
        part_ref[tile, 5] = faces[0] + 0.25 * TIME_STEP * (plus_z(y_pair) - minus_z(y_pair))
        part_ref[tile, 6] = faces[1]
        part_ref[tile, 7] = faces[2] - 0.25 * TIME_STEP * (y_across + minus_z(y_across))
        emf_ref[tile, 0] = z_here + z_lower
        emf_ref[tile, 1] = (plus_z(emf_x) - x_below) - (z_upper - z_lower)
        emf_ref[tile, 2] = emf_x + x_below

    for tile in range(9):
        first(tile)

    def last(tile):
        before, after = (tile + 8) % 9, tile + 1
        rows, columns = pl.ds(row, 8), pl.ds(tile * TILE, TILE)
        for n, field in enumerate((0, 1, 2, 3, 7)):
            flux = flux_ref[tile, n]
            out_ref[field, rows, columns] = part_ref[tile, n] - TIME_STEP * (
                plus_y(flux, flux_ref[after, n]) - flux
            )
        around = [
            (emf_ref[before, n], emf_ref[tile, n], emf_ref[after, n]) for n in range(3)
        ]
        across_z = plus_y(around[0][1], around[0][2]) - minus_y(around[0][0], around[0][1])
        pair = around[1][1] + minus_y(around[1][0], around[1][1])
        across_x = plus_y(around[2][1], around[2][2]) - minus_y(around[2][0], around[2][1])
        out_ref[4, rows, columns] = part_ref[tile, 5] - 0.25 * TIME_STEP * across_z
        out_ref[5, rows, columns] = part_ref[tile, 6] - 0.25 * TIME_STEP * pair
        out_ref[6, rows, columns] = part_ref[tile, 7] + 0.25 * TIME_STEP * across_x

    for tile in range(8):
        last(tile)


def per_device(state, row_shift, row_frac, edge_shift, edge_frac):
    tiles = state.reshape(FIELDS, ROWS // 8, 8, COLUMNS // TILE, TILE).transpose(0, 1, 3, 2, 4)
    tiles = tiles.reshape(FIELDS * ROWS * 8, TILE)
    dma, smem = pltpu.SemaphoreType.DMA, pltpu.SMEM

    def vmem(*shape):
        return pltpu.VMEM(shape, jnp.float32)

    return pl.pallas_call(
        kernel,
        out_shape=jax.ShapeDtypeStruct((FIELDS, ROWS, COLUMNS), jnp.float32),
        in_specs=[pl.BlockSpec(memory_space=pltpu.HBM)] * 5,
        out_specs=pl.BlockSpec(memory_space=pltpu.HBM),
        scratch_shapes=[
            vmem(*tiles.shape),
            smem(row_shift.shape, jnp.int32), smem(row_frac.shape, jnp.float32),
            smem((1,), jnp.int32), smem((1,), jnp.float32),
            vmem(ROWS, 2, HELD, 8, TILE),
            vmem(GHOSTS, 8, TILE),
            vmem(HELD, TILES + PAD, TILE),
            vmem(HELD, TILES + PAD, TILE),
            vmem(TILES + PAD, TILE),
            vmem(2, RING, LINES, TILE),
            vmem(RING, 16, TILE),
            vmem(SLOTS * 2 * LINES, TILE),
            vmem(GHOSTS * 16, TILE),
            vmem(FIELDS, ROWS, COLUMNS),
            vmem(9, 5, 8, TILE), vmem(9, 8, 8, TILE), vmem(9, 3, 8, TILE),
            dma((5,)), dma, dma, dma, dma, dma((2,)), dma, dma((2,)), dma, dma,
        ],
        compiler_params=pltpu.CompilerParams(
            collective_id=0, has_side_effects=True, vmem_limit_bytes=VMEM_LIMIT
        ),
        name="step",
    )(tiles, row_shift, row_frac, edge_shift, edge_frac)


def solution(mesh):
    return jax.shard_map(
        per_device,
        mesh=mesh,
        in_specs=(P(None, "rad", "az"), P(), P(), P(), P()),
        out_specs=P(None, "rad", "az"),
        check_vma=False,
    )
```

time: 53.2 us -> 47 us (0.88)
  the two profiles are of different devices: /device:TPU:34 before, /device:TPU:1 now
where the time goes in v3:
time: 47 us; the launch traced here: 46.8 us
  Pallas kernels  43.2 us (92%)
  local copies, waits for them, and re-layouts  2.31 us (5%)
  between operations  1.3 us (3%)
    pallas_call x1, Pallas kernels, per_device(): pl.pallas_call(kernel, out_shape=jax.ShapeDtypeStruct((FIELDS, ROWS, COLU...  43.2 us
    unnamed x1, local copies, waits for them, and re-layouts  2.31 us

profile of v3, /device:TPU:1, one launch (start us, length us, event | category | flops | bytes accessed | tf_op | source)
XLA Modules:
  0.0 46.8 jit_solution(3318571115451200933)
XLA Ops:
  1.3 43.2 %step.1 = f32[8,32,1024]{2,1,0:T(8,128)} custom-call(f32[2048,128]{1,0:T(8,128)} %bitcast.5, s32[128]{0:T(128)} %shift_hbm.1, f32[128]{0:T(128)} %frac_hbm.1, s32[1]{0:T(128)S(6)} %copy.7.edge_shift_hbm, f32[1]{0:T(128)S(6)} %copy.8.edge_frac_hbm), custom_call_target="tpu_custom_call" | custom-call | tf_op jit(solution)/shard_map/step/pallas_call | solution.py:470
  44.5 2.3 %copy.9 = f32[8,32,1024]{2,1,0:T(8,128)} copy(f32[8,32,1024]{2,1,0:T(8,128)} %step.1) | data formatting | bytes 2097152

commit v4 on v3

--- a/solution.py
+++ b/solution.py
@@ -8,17 +8,20 @@
 MESH = pl.DeviceIdType.MESH
 NZ = 32
 FIELDS = 8
-HELD = 4
+HELD = 2
+PIECES = 4
+PARTS = 4
+GROUPED = 4
 ROWS = 32
-HALF = 16
 COLUMNS = 1024
 RING = 32
 TILE = 128
 TILES = RING * COLUMNS // TILE
 PAD = 24
-WINDOW = 36
-LINES = 40
-SLOTS = ROWS + 3
+WINDOW = 18
+LINES = 24
+SLOTS = (6, 8)
+BX_PIECE = 2
 GHOSTS = 17
 VMEM_LIMIT = 60 * 2**20
 TIME_STEP = 0.2
@@ -29,37 +32,52 @@
     return az // 8, (az // 4) % 2, az % 4, rad // 2, rad % 2
 
 
-def holder_of(group, index):
-    i = index % 16
+def row_of(part, first):
+    last = first == 7
+    if part == 0:
+        return jnp.where(last, 3, 0), first
+    return part - jnp.where(last, 1, 0), first
+
+
+def ghost_holder(n):
+    i = 2 if n == 16 else n % 8 // 2 * 4 + n % 2
+    group = 0 if n < 8 else 3
     low = (group % 2 + i // 4 + (i // 2) % 2) % 2
-    return {"az": 2 * i + low, "rad": (1 - group // 2) * 2 + index // 16}
+    return {"az": 2 * i + low, "rad": 2 if n < 8 else 1}
 
 
 def ghost_source(n):
     if n < 8:
-        return ROWS - 1, n, 2 * n
+        return ROWS - 1, n
     if n < 16:
-        return 0, n - 8, 2 * n
-    return 1, 4, 17
+        return 0, n - 8
+    return 1, 4
 
 
 def kernel(
     state_hbm, shift_hbm, frac_hbm, edge_shift_hbm, edge_frac_hbm,
     out_hbm,
     state_ref, shift_ref, frac_ref, edge_shift_ref, edge_frac_ref,
-    rows_ref, strips_ref, held_low_ref, held_high_ref, strip_held_ref, moved_ref, moved_strip_ref, cells_ref, ghosts_ref,
+    rows_ref, strips_ref, held_0_ref, held_1_ref, held_2_ref, held_3_ref, strip_held_ref,
+    moved_ref, moved_strip_ref, cells_ref, ghosts_ref,
     out_ref, flux_ref, part_ref, emf_ref,
-    in_sem, rows_sem, strips_sem, back_sem, ghosts_back_sem, held_sem, strip_held_sem, row_sem, ghosts_sem, done_sem,
+    in_sem, rows_sem, strips_sem, back_sem, ghosts_back_sem, held_sem, strip_held_sem, row_sem, ghosts_sem,
+    hand_sem, handed_sem, done_sem,
 ):
     x, y_hi, z, y_lo, core = place()
     az, rad = lax.axis_index("az"), lax.axis_index("rad")
     parity = (x + y_hi + z) % 2
     group = (1 - y_lo) * 2 + parity
     index = core * 16 + az // 2
-    ghost = jnp.where(index == 17, 16, index // 2)
-    has_ghost = jnp.logical_or(index % 2 == 0, index == 17)
-    from_below = ghost < 8
-    ghost_group = jnp.where(from_below, (group + 3) % 4, (group + 1) % 4)
+    piece, first_row = index // 8, index % 8
+    held_refs = (held_0_ref, held_1_ref, held_2_ref, held_3_ref)
+    among = index % 16
+    for_inner = jnp.logical_and(jnp.logical_and(group == 0, core == 0), among % 4 < 2)
+    for_outer = jnp.logical_and(
+        jnp.logical_and(group == 3, core == 1), jnp.logical_or(among % 4 < 2, among == 2)
+    )
+    has_ghost = jnp.logical_or(for_inner, for_outer)
+    ghost = jnp.where(among == 2, 16, among // 4 * 2 + among % 4 + jnp.where(for_outer, 8, 0))
 
     loads = [
         pltpu.make_async_copy(source, target, in_sem.at[n])
@@ -75,68 +93,86 @@
 
     barrier = pltpu.get_barrier_semaphore()
 
-    def greet(target_group):
-        def one(d, carry):
-            pl.semaphore_signal(
-                barrier, inc=1, device_id={"az": d, "rad": target_group}, device_id_type=MESH
-            )
-            return carry
-
-        lax.fori_loop(0, RING, one, 0)
-
-    greet(group)
+    def greet(target_az, target_rad):
+        pl.semaphore_signal(
+            barrier, inc=1, device_id={"az": target_az, "rad": target_rad}, device_id_type=MESH
+        )
+
+    for d in range(RING):
+        greet(d, group)
+
+    @pl.when(rad > 0)
+    def _():
+        greet(az, rad - 1)
+
+    @pl.when(rad < 3)
+    def _():
+        greet(az, rad + 1)
 
     @pl.when(has_ghost)
     def _():
-        greet(ghost_group)
+        for d in range(RING):
+            greet(d, 3 - group)
 
     for load in loads:
         load.wait()
 
-    def field_lines(field, r):
-        return state_ref[pl.ds(field * 256 + r // 8 * 64 + r % 8, 8, stride=8), :]
-
-    for n in range(GHOSTS):
-        r, field, _ = ghost_source(n)
-        strips_ref[n] = field_lines(field, r)
-    pl.semaphore_wait(barrier, RING + GHOSTS)
-
-    for n in range(GHOSTS):
-        pltpu.make_async_remote_copy(
-            src_ref=strips_ref.at[n],
-            dst_ref=strip_held_ref.at[pl.ds(pl.multiple_of(az * 8, 8), 8)],
-            send_sem=strips_sem,
-            recv_sem=strip_held_sem,
-            device_id=holder_of((rad + (1 if n < 8 else 3)) % 4, ghost_source(n)[2]),
-            device_id_type=MESH,
-        ).start()
-
-    offset_parity = (core + parity) % 2
-    held_refs = (held_low_ref, held_high_ref)
-
-    def send_out(half):
-        def one(k, carry):
-            part, i = k // 16, k % 16
-            dx, dz = i % 4, (i // 4 + i) % 4
-            dy = (offset_parity + dx + dz) % 2
-            target = ((x + dx) % 4) * 8 + ((y_hi + dy) % 2) * 4 + (z + dz) % 4
-            r = half * HALF + target // 2
-            for f in range(HELD):
-                rows_ref[r, part, f] = field_lines(part * HELD + f, r)
+    def field_lines(field, row):
+        eighth, rest = row if isinstance(row, tuple) else (row // 8, row % 8)
+        return state_ref[pl.ds(field * 256 + eighth * 64 + rest, 8, stride=8), :]
+
+    pl.semaphore_wait(barrier, RING + jnp.where(rad == 0, 10, jnp.where(rad == 3, 9, 2)))
+
+    my_lines = pl.ds(pl.multiple_of(az * 8, 8), 8)
+
+    def send_strips(ghosts):
+        for n in ghosts:
+            r, field = ghost_source(n)
+            strips_ref[n] = field_lines(field, r)
             pltpu.make_async_remote_copy(
-                src_ref=rows_ref.at[r, part],
-                dst_ref=held_refs[half].at[:, pl.ds(pl.multiple_of(az * 8, 8), 8)],
-                send_sem=rows_sem,
-                recv_sem=held_sem.at[half],
-                device_id={"az": target, "rad": (1 - y_lo) * 2 + part},
+                src_ref=strips_ref.at[n],
+                dst_ref=strip_held_ref.at[my_lines],
+                send_sem=strips_sem,
+                recv_sem=strip_held_sem,
+                device_id=ghost_holder(n),
                 device_id_type=MESH,
             ).start()
+
+    pl.when(rad == 3)(lambda: send_strips(range(8)))
+    pl.when(rad == 0)(lambda: send_strips(range(8, GHOSTS)))
+    offset_parity = (core + parity) % 2
+
+    def send_out(part):
+        def some(j, carry):
+            sends = []
+            for m in range(GROUPED):
+                k = j * GROUPED + m
+                side, i = k // 16, k % 16
+                dx, dz = i % 4, (i // 4 + i) % 4
+                dy = (offset_parity + dx + dz) % 2
+                target = ((x + dx) % 4) * 8 + ((y_hi + dy) % 2) * 4 + (z + dz) % 4
+                to_piece, first = side * 2 + target // 16, target // 2 % 8
+                row = row_of(part, first)
+                for f in range(HELD):
+                    rows_ref[to_piece, first, part, f] = field_lines(to_piece * HELD + f, row)
+                sends.append(
+                    pltpu.make_async_remote_copy(
+                        src_ref=rows_ref.at[to_piece, first, part],
+                        dst_ref=held_refs[part].at[:, my_lines],
+                        send_sem=rows_sem,
+                        recv_sem=held_sem.at[part],
+                        device_id={"az": target, "rad": (1 - y_lo) * 2 + side},
+                        device_id_type=MESH,
+                    )
+                )
+            for send in sends:
+                send.start()
             return carry
 
-        lax.fori_loop(0, RING, one, 0)
-
-    send_out(0)
-    send_out(1)
+        lax.fori_loop(0, RING // GROUPED, some, 0)
+
+    for part in range(PARTS):
+        send_out(part)
 
     def same_size(ref, send_sem, recv_sem):
         return pltpu.make_async_remote_copy(
@@ -167,87 +203,14 @@
             outer = term if outer is None else outer + term
         return inner, outer
 
-    def send_back(half):
-        held_ref = held_refs[half]
-        same_size(held_ref.at[:, :TILES], rows_sem, held_sem.at[half]).wait_recv()
-        for f in range(HELD):
-            held_ref[f, TILES:] = held_ref[f, :PAD]
-        r = half * HALF + az // 2
-        shift, fraction = shift_ref[group * ROWS + r], frac_ref[group * ROWS + r]
-        whole, taps = taps_of(shift, (1.0 - fraction, fraction))
-
-        def fill(d):
-            base = lax.rem(8 * d + 2 * TILES - 3 - whole, TILES)
-            inner, outer = blend(
-                taps,
-                lambda f, n: held_ref[f, pl.ds(base + n, 8), :],
-                lambda n: jnp.concatenate(
-                    [held_ref[f, pl.ds(base + n, 1), :] for f in range(HELD)] * 2, axis=0
-                ),
-                HELD,
-            )
-            for f in range(HELD):
-                moved_ref[half, d, f * 8 : f * 8 + 8] = inner[f]
-            moved_ref[half, d, 32:LINES] = outer
-
-        if half == 0:
-            strip_whole, strip_taps = ghost_taps()
-
-        def fill_strip(d):
-            base = lax.rem(8 * d + 2 * TILES - 3 - strip_whole, TILES)
-            lines = lambda n: strip_held_ref[pl.ds(base + n, 8), :]
-            inner, outer = blend(strip_taps, lambda f, n: lines(n), lines, 1)
-            moved_strip_ref[d, 0:8] = inner[0]
-            moved_strip_ref[d, 8:16] = outer
-
-        def one(k, carry):
-            dx, dz, dy = k % 4, (k // 4 + k) % 4, (k // 16 + k) % 2
-            d = ((x + dx) % 4) * 8 + ((y_hi + dy) % 2) * 4 + (z + dz) % 4
-            fill(d)
-            pltpu.make_async_remote_copy(
-                src_ref=moved_ref.at[half, d, :WINDOW],
-                dst_ref=cells_ref.at[pl.ds(pl.multiple_of(((r + 1) * 2 + core) * LINES, 8), WINDOW)],
-                send_sem=back_sem,
-                recv_sem=row_sem.at[half],
-                device_id={"az": d, "rad": group},
-                device_id_type=MESH,
-            ).start()
-
-            if half == 0:
-                @pl.when(has_ghost)
-                def _():
-                    fill_strip(d)
-                    pltpu.make_async_remote_copy(
-                        src_ref=moved_strip_ref.at[d, :9],
-                        dst_ref=ghosts_ref.at[pl.ds(pl.multiple_of(ghost * 16, 16), 9)],
-                        send_sem=ghosts_back_sem,
-                        recv_sem=ghosts_sem,
-                        device_id={"az": d, "rad": group},
-                        device_id_type=MESH,
-                    ).start()
-
-            return carry
-
-        lax.fori_loop(0, RING, one, 0)
+    odd = lax.broadcasted_iota(jnp.int32, (8, TILE), 0) % 2 == 1
 
     def ghost_taps():
-        @pl.when(has_ghost)
-        def _():
-            same_size(strip_held_ref.at[:TILES], strips_sem, strip_held_sem).wait_recv()
-            strip_held_ref[TILES:, :] = strip_held_ref[:PAD, :]
-
-        source_row = ghost_group * ROWS + jnp.where(from_below, ROWS - 1, ghost // 16)
+        source_row = jnp.where(for_inner, ROWS * 4 - 1, ghost // 16)
         shift, fraction = shift_ref[source_row], frac_ref[source_row]
         edge_shift, edge_frac = edge_shift_ref[0], edge_frac_ref[0]
-        at_low, at_high = group == 0, group == 3
-        more = jnp.where(
-            from_below,
-            jnp.where(at_low, edge_shift, 0),
-            jnp.where(at_high, RING * COLUMNS // NZ - 1 - edge_shift, 0),
-        )
-        edge = jnp.where(
-            from_below, jnp.where(at_low, edge_frac, 0.0), jnp.where(at_high, 1.0 - edge_frac, 0.0)
-        )
+        more = jnp.where(for_inner, edge_shift, RING * COLUMNS // NZ - 1 - edge_shift)
+        edge = jnp.where(for_inner, edge_frac, 1.0 - edge_frac)
         return taps_of(
             lax.rem(shift + more, RING * COLUMNS // NZ),
             (
@@ -257,8 +220,135 @@
             ),
         )
 
-    send_back(0)
-    send_back(1)
+    def target(k):
+        dx, dz, dy = k % 4, (k // 4 + k) % 4, (k // 16 + k) % 2
+        return ((x + dx) % 4) * 8 + ((y_hi + dy) % 2) * 4 + (z + dz) % 4
+
+    def first_tile(d, whole):
+        return lax.rem(8 * d + 2 * TILES - 3 - whole, TILES)
+
+    def send_back(part):
+        held_ref = held_refs[part]
+        same_size(held_ref.at[:, :TILES], rows_sem, held_sem.at[part]).wait_recv()
+        for f in range(HELD):
+            held_ref[f, TILES:] = held_ref[f, :PAD]
+        eighth, rest = row_of(part, first_row)
+        r = group * ROWS + eighth * 8 + rest
+        shift, fraction = shift_ref[r], frac_ref[r]
+        whole, taps = taps_of(shift, (1.0 - fraction, fraction))
+
+        def fill(d):
+            base = first_tile(d, whole)
+
+            def halo_lines(n):
+                pair = [
+                    jnp.broadcast_to(held_ref[f, pl.ds(base + n, 1), :], (8, TILE))
+                    for f in range(HELD)
+                ]
+                return jnp.where(odd, pair[1], pair[0])
+
+            inner, outer = blend(
+                taps, lambda f, n: held_ref[f, pl.ds(base + n, 8), :], halo_lines, HELD
+            )
+            for f in range(HELD):
+                moved_ref[part, d, f * 8 : f * 8 + 8] = inner[f]
+            moved_ref[part, d, HELD * 8 :] = outer
+
+        def some(j, carry):
+            ds = [target(j * GROUPED + m) for m in range(GROUPED)]
+            for d in ds:
+                fill(d)
+            for d in ds:
+                pltpu.make_async_remote_copy(
+                    src_ref=moved_ref.at[part, d, :WINDOW],
+                    dst_ref=cells_ref.at[eighth + 1, rest, piece, :WINDOW],
+                    send_sem=back_sem,
+                    recv_sem=row_sem.at[part],
+                    device_id={"az": d, "rad": group},
+                    device_id_type=MESH,
+                ).start()
+            return carry
+
+        lax.fori_loop(0, RING // GROUPED, some, 0)
+
+    def send_ghosts():
+        same_size(strip_held_ref.at[:TILES], strips_sem, strip_held_sem).wait_recv()
+        strip_held_ref[TILES:, :] = strip_held_ref[:PAD, :]
+        whole, taps = ghost_taps()
+
+        def fill(d):
+            base = first_tile(d, whole)
+            lines = lambda n: strip_held_ref[pl.ds(base + n, 8), :]
+            inner, outer = blend(taps, lambda f, n: lines(n), lines, 1)
+            moved_strip_ref[d, 0:8] = inner[0]
+            moved_strip_ref[d, 8:16] = outer
+
+        def some(j, carry):
+            ds = [target(j * GROUPED + m) for m in range(GROUPED)]
+            for d in ds:
+                fill(d)
+            for d in ds:
+                pltpu.make_async_remote_copy(
+                    src_ref=moved_strip_ref.at[d, :9],
+                    dst_ref=ghosts_ref.at[pl.ds(pl.multiple_of(ghost * 16, 16), 9)],
+                    send_sem=ghosts_back_sem,
+                    recv_sem=ghosts_sem,
+                    device_id={"az": d, "rad": group},
+                    device_id_type=MESH,
+                ).start()
+            return carry
+
+        lax.fori_loop(0, RING // GROUPED, some, 0)
+
+    for part in range(PARTS):
+        send_back(part)
+        if part == 0:
+            pl.when(has_ghost)(send_ghosts)
+
+    def arrived(part):
+        same_size(cells_ref.at[1, :, :, :WINDOW], back_sem, row_sem.at[part]).wait_recv()
+
+    def hand(source, slot, n, neighbour):
+        return pltpu.make_async_remote_copy(
+            src_ref=source,
+            dst_ref=slot,
+            send_sem=hand_sem.at[n],
+            recv_sem=handed_sem.at[n],
+            device_id={"az": az, "rad": neighbour},
+            device_id_type=MESH,
+        )
+
+    to_outer = [hand(cells_ref.at[4, 7, :, :WINDOW], cells_ref.at[0, 7, :, :WINDOW], 0, (rad + 1) % 4)]
+    to_inner = [
+        hand(cells_ref.at[1, 0, :, :WINDOW], cells_ref.at[5, 0, :, :WINDOW], 1, (rad + 3) % 4),
+        hand(cells_ref.at[1, 1, BX_PIECE, :WINDOW], cells_ref.at[5, 1, BX_PIECE, :WINDOW], 2, (rad + 3) % 4),
+    ]
+    arrived(0)
+
+    @pl.when(rad < 3)
+    def _():
+        for copy in to_outer:
+            copy.start()
+
+    @pl.when(rad > 0)
+    def _():
+        for copy in to_inner:
+            copy.start()
+
+    lines_ref = cells_ref.reshape(SLOTS[0] * SLOTS[1] * PIECES * LINES, TILE)
+
+    def take_ghosts(ghosts):
+        same_size(ghosts_ref.at[: len(ghosts) * 9], ghosts_back_sem, ghosts_sem).wait_recv()
+        for n in ghosts:
+            row, field = (-1, n) if n < 8 else (ROWS, n - 8) if n < 16 else (ROWS + 1, 4)
+            first = ((row + 8) * PIECES + field // HELD) * LINES
+            at, ninth = first + field % HELD * 8, first + HELD * 8 + field % HELD
+            lines_ref[at : at + 8, :] = ghosts_ref[n * 16 : n * 16 + 8]
+            lines_ref[ninth : ninth + 1, :] = ghosts_ref[n * 16 + 8 : n * 16 + 9]
+
+    def received(copies):
+        for copy in copies:
+            copy.wait_recv()
 
     def finish(block):
         return pltpu.make_async_copy(
@@ -267,35 +357,51 @@
             done_sem,
         )
 
-    def arrived(half):
-        same_size(cells_ref.at[: HALF * 2 * WINDOW], back_sem, row_sem.at[half]).wait_recv()
-
-    arrived(0)
-    same_size(ghosts_ref.at[: GHOSTS * 9], ghosts_back_sem, ghosts_sem).wait_recv()
-    for n in range(GHOSTS):
-        slot, field = ((0, n) if n < 8 else (ROWS + 1, n - 8) if n < 16 else (ROWS + 2, 4))
-        first = (slot * 2 + field // HELD) * LINES
-        at = first + field % HELD * 8
-        cells_ref[at : at + 8] = ghosts_ref[n * 16 : n * 16 + 8]
-        cells_ref[first + 32 + field % HELD : first + 33 + field % HELD] = ghosts_ref[n * 16 + 8 : n * 16 + 9]
-    step_block(cells_ref, out_ref, flux_ref, part_ref, emf_ref, 0)
-    finish(0).start()
-    arrived(1)
-
-    def later(block, carry):
-        step_block(cells_ref, out_ref, flux_ref, part_ref, emf_ref, block)
+    def one(block, carry):
+        @pl.when(block == 0)
+        def _():
+            arrived(1)
+            pl.when(rad > 0)(lambda: received(to_outer))
+            pl.when(rad == 0)(lambda: take_ghosts(range(8)))
+
+        pl.when(block == 1)(lambda: arrived(2))
+
+        @pl.when(block == 2)
+        def _():
+            arrived(3)
+            pl.when(rad < 3)(lambda: received(to_inner))
+            pl.when(rad == 3)(lambda: take_ghosts(range(8, GHOSTS)))
+
+        step_block(lines_ref, out_ref, flux_ref, part_ref, emf_ref, block)
         finish(block).start()
         return carry
 
-    lax.fori_loop(1, ROWS // 8, later, 0)
+    lax.fori_loop(0, ROWS // 8, one, 0)
 
     same_size(rows_ref, rows_sem, held_sem.at[0]).wait_send()
-    same_size(strips_ref, strips_sem, held_sem.at[0]).wait_send()
     same_size(moved_ref.at[:, :, :WINDOW], back_sem, held_sem.at[0]).wait_send()
 
+    @pl.when(rad == 3)
+    def _():
+        same_size(strips_ref.at[:8], strips_sem, held_sem.at[0]).wait_send()
+
+    @pl.when(rad == 0)
+    def _():
+        same_size(strips_ref.at[8:GHOSTS], strips_sem, held_sem.at[0]).wait_send()
+
     @pl.when(has_ghost)
     def _():
         same_size(moved_strip_ref.at[:, :9], ghosts_back_sem, held_sem.at[0]).wait_send()
+
+    @pl.when(rad < 3)
+    def _():
+        for copy in to_outer:
+            copy.wait_send()
+
+    @pl.when(rad > 0)
+    def _():
+        for copy in to_inner:
+            copy.wait_send()
 
     pltpu.make_async_copy(out_ref, out_hbm, done_sem).wait()
 
@@ -335,9 +441,9 @@
     down = jnp.where(level == 0, lane + (NZ - 1), lane - 1)
 
     def load(field, row, tile):
-        line = field % HELD * 8 + tile if tile < 8 else 32 + field % HELD
-        first = ((row + 1) * 2 + field // HELD) * LINES + line
-        return cells_ref[pl.ds(first, 8, stride=2 * LINES), :]
+        line = field % HELD * 8 + tile if tile < 8 else HELD * 8 + field % HELD
+        first = ((row + 8) * PIECES + field // HELD) * LINES + line
+        return cells_ref[pl.ds(first, 8, stride=PIECES * LINES), :]
 
     def plus_z(v):
         return jnp.take_along_axis(v, up, axis=1, mode="promise_in_bounds")
@@ -476,18 +582,17 @@
             vmem(*tiles.shape),
             smem(row_shift.shape, jnp.int32), smem(row_frac.shape, jnp.float32),
             smem((1,), jnp.int32), smem((1,), jnp.float32),
-            vmem(ROWS, 2, HELD, 8, TILE),
+            vmem(PIECES, 8, PARTS, HELD, 8, TILE),
             vmem(GHOSTS, 8, TILE),
-            vmem(HELD, TILES + PAD, TILE),
-            vmem(HELD, TILES + PAD, TILE),
+            *[vmem(HELD, TILES + PAD, TILE)] * PARTS,
             vmem(TILES + PAD, TILE),
-            vmem(2, RING, LINES, TILE),
+            vmem(PARTS, RING, LINES, TILE),
             vmem(RING, 16, TILE),
-            vmem(SLOTS * 2 * LINES, TILE),
+            vmem(*SLOTS, PIECES, LINES, TILE),
             vmem(GHOSTS * 16, TILE),
             vmem(FIELDS, ROWS, COLUMNS),
             vmem(9, 5, 8, TILE), vmem(9, 8, 8, TILE), vmem(9, 3, 8, TILE),
-            dma((5,)), dma, dma, dma, dma, dma((2,)), dma, dma((2,)), dma, dma,
+            dma((5,)), dma, dma, dma, dma, dma((PARTS,)), dma, dma((PARTS,)), dma, dma((3,)), dma((3,)), dma,
         ],
         compiler_params=pltpu.CompilerParams(
             collective_id=0, has_side_effects=True, vmem_limit_bytes=VMEM_LIMIT

time: 47 us -> 44.5 us (0.947)
  Pallas kernels: 43.2 us -> 40.6 us
    pallas_call x1, Pallas kernels: 43.2 us -> 40.6 us  [per_device(): pl.pallas_call(kernel, out_shape=jax.ShapeDtypeStruct((FIELDS, ROWS, COLU...]
where the time goes in v4:
time: 44.5 us; the launch traced here: 44.3 us
  Pallas kernels  40.6 us (91%)
  local copies, waits for them, and re-layouts  2.31 us (5%)
  between operations  1.3 us (3%)
    pallas_call x1, Pallas kernels, per_device(): pl.pallas_call(kernel, out_shape=jax.ShapeDtypeStruct((FIELDS, ROWS, COLU...  40.6 us
    unnamed x1, local copies, waits for them, and re-layouts  2.31 us

profile of v4, /device:TPU:1, one launch (start us, length us, event | category | flops | bytes accessed | tf_op | source)
XLA Modules:
  0.0 44.3 jit_solution(10372925923223206911)
XLA Ops:
  1.3 40.6 %step.1 = f32[8,32,1024]{2,1,0:T(8,128)} custom-call(f32[2048,128]{1,0:T(8,128)} %bitcast.5, s32[128]{0:T(128)} %shift_hbm.1, f32[128]{0:T(128)} %frac_hbm.1, s32[1]{0:T(128)S(6)} %copy.7.edge_shift_hbm, f32[1]{0:T(128)S(6)} %copy.8.edge_frac_hbm), custom_call_target="tpu_custom_call" | custom-call | tf_op jit(solution)/shard_map/step/pallas_call | solution.py:576
  41.9 2.3 %copy.9 = f32[8,32,1024]{2,1,0:T(8,128)} copy(f32[8,32,1024]{2,1,0:T(8,128)} %step.1) | data formatting | bytes 2097152

commit v5 on v4

--- a/solution.py
+++ b/solution.py
@@ -23,7 +23,7 @@
 SLOTS = (6, 8)
 BX_PIECE = 2
 GHOSTS = 17
-VMEM_LIMIT = 60 * 2**20
+VMEM_LIMIT = 28 * 2**20
 TIME_STEP = 0.2
 
 
@@ -55,14 +55,14 @@
 
 
 def kernel(
-    state_hbm, shift_hbm, frac_hbm, edge_shift_hbm, edge_frac_hbm,
-    out_hbm,
-    state_ref, shift_ref, frac_ref, edge_shift_ref, edge_frac_ref,
+    state_hbm, shift_hbm, frac_hbm, edge_shift_ref, edge_frac_ref,
+    out_ref,
+    state_ref, shift_ref, frac_ref,
     rows_ref, strips_ref, held_0_ref, held_1_ref, held_2_ref, held_3_ref, strip_held_ref,
     moved_ref, moved_strip_ref, cells_ref, ghosts_ref,
-    out_ref, flux_ref, part_ref, emf_ref,
+    flux_ref, part_ref, emf_ref,
     in_sem, rows_sem, strips_sem, back_sem, ghosts_back_sem, held_sem, strip_held_sem, row_sem, ghosts_sem,
-    hand_sem, handed_sem, done_sem,
+    hand_sem, handed_sem,
 ):
     x, y_hi, z, y_lo, core = place()
     az, rad = lax.axis_index("az"), lax.axis_index("rad")
@@ -82,10 +82,7 @@
     loads = [
         pltpu.make_async_copy(source, target, in_sem.at[n])
         for n, (source, target) in enumerate(
-            (
-                (state_hbm, state_ref), (shift_hbm, shift_ref), (frac_hbm, frac_ref),
-                (edge_shift_hbm, edge_shift_ref), (edge_frac_hbm, edge_frac_ref),
-            )
+            ((state_hbm, state_ref), (shift_hbm, shift_ref), (frac_hbm, frac_ref))
         )
     ]
     for load in loads:
@@ -350,13 +347,6 @@
         for copy in copies:
             copy.wait_recv()
 
-    def finish(block):
-        return pltpu.make_async_copy(
-            out_ref.at[:, pl.ds(pl.multiple_of(block * 8, 8), 8)],
-            out_hbm.at[:, pl.ds(pl.multiple_of(block * 8, 8), 8)],
-            done_sem,
-        )
-
     def one(block, carry):
         @pl.when(block == 0)
         def _():
@@ -373,7 +363,6 @@
             pl.when(rad == 3)(lambda: take_ghosts(range(8, GHOSTS)))
 
         step_block(lines_ref, out_ref, flux_ref, part_ref, emf_ref, block)
-        finish(block).start()
         return carry
 
     lax.fori_loop(0, ROWS // 8, one, 0)
@@ -402,8 +391,6 @@
     def _():
         for copy in to_inner:
             copy.wait_send()
-
-    pltpu.make_async_copy(out_ref, out_hbm, done_sem).wait()
 
 
 def side(cell, normal, face):
@@ -576,12 +563,11 @@
     return pl.pallas_call(
         kernel,
         out_shape=jax.ShapeDtypeStruct((FIELDS, ROWS, COLUMNS), jnp.float32),
-        in_specs=[pl.BlockSpec(memory_space=pltpu.HBM)] * 5,
-        out_specs=pl.BlockSpec(memory_space=pltpu.HBM),
+        in_specs=[pl.BlockSpec(memory_space=pltpu.HBM)] * 3 + [pl.BlockSpec(memory_space=pltpu.SMEM)] * 2,
+        out_specs=pl.BlockSpec(memory_space=pltpu.VMEM),
         scratch_shapes=[
             vmem(*tiles.shape),
             smem(row_shift.shape, jnp.int32), smem(row_frac.shape, jnp.float32),
-            smem((1,), jnp.int32), smem((1,), jnp.float32),
             vmem(PIECES, 8, PARTS, HELD, 8, TILE),
             vmem(GHOSTS, 8, TILE),
             *[vmem(HELD, TILES + PAD, TILE)] * PARTS,
@@ -590,15 +576,18 @@
             vmem(RING, 16, TILE),
             vmem(*SLOTS, PIECES, LINES, TILE),
             vmem(GHOSTS * 16, TILE),
-            vmem(FIELDS, ROWS, COLUMNS),
             vmem(9, 5, 8, TILE), vmem(9, 8, 8, TILE), vmem(9, 3, 8, TILE),
-            dma((5,)), dma, dma, dma, dma, dma((PARTS,)), dma, dma((PARTS,)), dma, dma((3,)), dma((3,)), dma,
+            dma((3,)), dma, dma, dma, dma, dma((PARTS,)), dma, dma((PARTS,)), dma, dma((3,)), dma((3,)),
         ],
         compiler_params=pltpu.CompilerParams(
             collective_id=0, has_side_effects=True, vmem_limit_bytes=VMEM_LIMIT
         ),
         name="step",
-    )(tiles, row_shift, row_frac, edge_shift, edge_frac)
+    )(
+        *[pltpu.with_memory_space_constraint(a, pltpu.HBM) for a in (tiles, row_shift, row_frac)],
+        edge_shift,
+        edge_frac,
+    )
 
 
 def solution(mesh):

time: 44.5 us -> 42.4 us (0.953)
  local copies, waits for them, and re-layouts: 2.31 us -> 0.97 us
  Pallas kernels: 40.6 us -> 39.9 us
    unnamed x1, local copies, waits for them, and re-layouts: 2.31 us -> 0.97 us
    pallas_call x1, Pallas kernels: 40.6 us -> 39.9 us  [per_device(): pl.pallas_call(kernel, out_shape=jax.ShapeDtypeStruct((FIELDS, ROWS, COLU...]
where the time goes in v5:
time: 42.4 us; the launch traced here: 42.2 us
  Pallas kernels  39.9 us (94%)
  between operations  1.3 us (3%)
  local copies, waits for them, and re-layouts  0.97 us (2%)
    pallas_call x1, Pallas kernels, per_device(): pl.pallas_call(kernel, out_shape=jax.ShapeDtypeStruct((FIELDS, ROWS, COLU...  39.9 us
    unnamed x1, local copies, waits for them, and re-layouts  0.97 us

profile of v5, /device:TPU:1, one launch (start us, length us, event | category | flops | bytes accessed | tf_op | source)
XLA Modules:
  0.0 42.2 jit_solution(15258950813514587767)
XLA Ops:
  1.3 39.9 %step.1 = f32[8,32,1024]{2,1,0:T(8,128)S(1)} custom-call(f32[2048,128]{1,0:T(8,128)} %bitcast.5, s32[128]{0:T(128)} %shift_hbm.1, f32[128]{0:T(128)} %frac_hbm.1, s32[1]{0:T(128)S(6)} %copy.7.edge_shift_ref, f32[1]{0:T(128)S(6)} %copy.8.edge_frac_ref), custom_call_target="tpu_custom_call" | custom-call | tf_op jit(solution)/shard_map/step/pallas_call | solution.py:563
  41.2 1.0 %copy.9 = f32[8,32,1024]{2,1,0:T(8,128)} copy(f32[8,32,1024]{2,1,0:T(8,128)S(1)} %step.1) | data formatting | bytes 2097152

commit v6 on v5

--- a/solution.py
+++ b/solution.py
@@ -60,7 +60,7 @@
     state_ref, shift_ref, frac_ref,
     rows_ref, strips_ref, held_0_ref, held_1_ref, held_2_ref, held_3_ref, strip_held_ref,
     moved_ref, moved_strip_ref, cells_ref, ghosts_ref,
-    flux_ref, part_ref, emf_ref,
+    flux_ref, part_ref, emf_ref, cell_ref, side_ref,
     in_sem, rows_sem, strips_sem, back_sem, ghosts_back_sem, held_sem, strip_held_sem, row_sem, ghosts_sem,
     hand_sem, handed_sem,
 ):
@@ -347,12 +347,15 @@
         for copy in copies:
             copy.wait_recv()
 
+    before_first, step = stepper(lines_ref, out_ref, flux_ref, part_ref, emf_ref, cell_ref, side_ref)
+
     def one(block, carry):
         @pl.when(block == 0)
         def _():
             arrived(1)
             pl.when(rad > 0)(lambda: received(to_outer))
             pl.when(rad == 0)(lambda: take_ghosts(range(8)))
+            before_first()
 
         pl.when(block == 1)(lambda: arrived(2))
 
@@ -362,7 +365,7 @@
             pl.when(rad < 3)(lambda: received(to_inner))
             pl.when(rad == 3)(lambda: take_ghosts(range(8, GHOSTS)))
 
-        step_block(lines_ref, out_ref, flux_ref, part_ref, emf_ref, block)
+        step(block)
         return carry
 
     lax.fori_loop(0, ROWS // 8, one, 0)
@@ -421,7 +424,7 @@
     ]
 
 
-def step_block(cells_ref, out_ref, flux_ref, part_ref, emf_ref, block):
+def stepper(cells_ref, out_ref, flux_ref, part_ref, emf_ref, cell_ref, side_ref):
     lane = lax.broadcasted_iota(jnp.int32, (8, TILE), 1)
     level = lane % NZ
     up = jnp.where(level == NZ - 1, lane - (NZ - 1), lane + 1)
@@ -444,48 +447,84 @@
     def plus_y(v, after):
         return pltpu.roll(jnp.where(lane < NZ, after, v), TILE - NZ, 1)
 
-    def read(row, tile, after):
-        density = load(0, row, tile)
-        momenta = [load(n, row, tile) for n in (1, 2, 3)]
+    def lines_of(row):
+        return pl.ds(pl.multiple_of(row + 16, 8), 8)
+
+    def work_out(row):
+        for tile in range(9):
+            density = load(0, row + 1, tile)
+            faces = [load(n, row + 1, tile) for n in (4, 5, 6)]
+            c = [
+                0.5 * (faces[0] + load(4, row + 2, tile)),
+                0.5 * (faces[1] + plus_y(faces[1], load(5, row + 1, (tile + 1) % 9))),
+                0.5 * (faces[2] + plus_z(faces[2])),
+            ]
+            inverse = 1.0 / density
+            v = [load(n, row + 1, tile) * inverse for n in (1, 2, 3)]
+            emf = [v[2] * c[1] - v[1] * c[2], v[0] * c[2] - v[2] * c[0], v[1] * c[0] - v[0] * c[1]]
+            for n, value in enumerate([*c, inverse, *emf]):
+                cell_ref[tile, n, lines_of(row), :] = value
+
+    def known(n, row, tile):
+        return cell_ref[tile, n, pl.ds(row + 15, 8), :]
+
+    def cell_at(row, tile):
+        return (
+            load(0, row, tile),
+            [load(n, row, tile) for n in (1, 2, 3)],
+            [known(n, row, tile) for n in (0, 1, 2)],
+            load(7, row, tile),
+            known(3, row, tile),
+        )
+
+    def outer_flux(row, tile, cell):
+        flux = face_flux(cell, cell_at(row + 1, tile), 0, load(4, row + 1, tile))
+        for n in range(5):
+            side_ref[tile, n, lines_of(row), :] = flux[n]
+        return flux
+
+    def before_first():
+        work_out(-8)
+        for tile in range(8):
+            outer_flux(-8, tile, cell_at(-8, tile))
+
+    def first(row, tile):
+        before = (tile + 8) % 9
+        cell = cell_at(row, tile)
+        density, momenta, centred, tracer, inverse = cell
         faces = [load(n, row, tile) for n in (4, 5, 6)]
-        tracer = load(7, row, tile)
-        centred = [
-            0.5 * (faces[0] + load(4, row + 1, tile)),
-            0.5 * (faces[1] + plus_y(faces[1], load(5, row, after))),
-            0.5 * (faces[2] + plus_z(faces[2])),
-        ]
-        return (density, momenta, centred, tracer, 1.0 / density), faces
-
-    row = pl.multiple_of(block * 8, 8)
-
-    def first(tile):
-        before, after = (tile + 8) % 9, (tile + 1) % 9
-        lower, _ = read(row - 1, tile, after)
-        cell, faces = read(row, tile, after)
-        upper, upper_faces = read(row + 1, tile, after)
-        density, momenta, centred, tracer, inverse = cell
-
-        def shifted(field):
+
+        def behind_of(field):
             return minus_y(load(field, row, before), load(field, row, tile))
 
-        before_bz = shifted(6)
-        behind_density = shifted(0)
+        behind_density = behind_of(0)
         behind = (
             behind_density,
-            [shifted(n) for n in (1, 2, 3)],
-            [
-                minus_y(0.5 * (load(4, row, before) + load(4, row + 1, before)), centred[0]),
-                None,
-                0.5 * (before_bz + plus_z(before_bz)),
-            ],
-            shifted(7),
+            [behind_of(n) for n in (1, 2, 3)],
+            [minus_y(known(0, row, before), centred[0]), None, minus_y(known(2, row, before), centred[2])],
+            behind_of(7),
             1.0 / behind_density,
         )
         flux_y = face_flux(behind, cell, 1, faces[1])
         for n in range(5):
             flux_ref[tile, n] = flux_y[n]
-        flux_low = face_flux(lower, cell, 0, faces[0])
-        flux_high = face_flux(cell, upper, 0, upper_faces[0])
+
+        emf_x, z_here = known(4, row, tile), known(6, row, tile)
+        z_lower, z_upper = known(6, row - 1, tile), known(6, row + 1, tile)
+        x_below = minus_z(emf_x)
+        emf_ref[tile, 0] = z_here + z_lower
+        emf_ref[tile, 1] = (plus_z(emf_x) - x_below) - (z_upper - z_lower)
+        emf_ref[tile, 2] = emf_x + x_below
+        if tile == 8:
+            return
+        y_here, y_lower, y_upper = known(5, row, tile), known(5, row - 1, tile), known(5, row + 1, tile)
+        y_pair, y_across = y_here + y_lower, y_upper - y_lower
+        part_ref[tile, 5] = faces[0] + 0.25 * TIME_STEP * (plus_z(y_pair) - minus_z(y_pair))
+        part_ref[tile, 6] = faces[1]
+        part_ref[tile, 7] = faces[2] - 0.25 * TIME_STEP * (y_across + minus_z(y_across))
+
+        flux_high = outer_flux(row, tile, cell)
+        flux_low = [side_ref[tile, n, pl.ds(row + 15, 8), :] for n in range(5)]
         below = (
             minus_z(density),
             [minus_z(m) for m in momenta],
@@ -504,33 +543,7 @@
                 value = value - TIME_STEP * 0.5 * momenta[0]
             part_ref[tile, n] = value
 
-        def velocity(c):
-            return [m * c[4] for m in c[1]]
-
-        def emf_y(c, v):
-            return v[0] * c[2][2] - v[2] * c[2][0]
-
-        def emf_z(c, v):
-            return v[1] * c[2][0] - v[0] * c[2][1]
-
-        v_lower, v, v_upper = velocity(lower), velocity(cell), velocity(upper)
-        emf_x = v[2] * centred[1] - v[1] * centred[2]
-        y_lower, y_here, y_upper = emf_y(lower, v_lower), emf_y(cell, v), emf_y(upper, v_upper)
-        z_lower, z_here, z_upper = emf_z(lower, v_lower), emf_z(cell, v), emf_z(upper, v_upper)
-        x_below = minus_z(emf_x)
-        y_pair = y_here + y_lower
-        y_across = y_upper - y_lower
-        part_ref[tile, 5] = faces[0] + 0.25 * TIME_STEP * (plus_z(y_pair) - minus_z(y_pair))
-        part_ref[tile, 6] = faces[1]
-        part_ref[tile, 7] = faces[2] - 0.25 * TIME_STEP * (y_across + minus_z(y_across))
-        emf_ref[tile, 0] = z_here + z_lower
-        emf_ref[tile, 1] = (plus_z(emf_x) - x_below) - (z_upper - z_lower)
-        emf_ref[tile, 2] = emf_x + x_below
-
-    for tile in range(9):
-        first(tile)
-
-    def last(tile):
+    def last(row, tile):
         before, after = (tile + 8) % 9, tile + 1
         rows, columns = pl.ds(row, 8), pl.ds(tile * TILE, TILE)
         for n, field in enumerate((0, 1, 2, 3, 7)):
@@ -538,9 +551,7 @@
             out_ref[field, rows, columns] = part_ref[tile, n] - TIME_STEP * (
                 plus_y(flux, flux_ref[after, n]) - flux
             )
-        around = [
-            (emf_ref[before, n], emf_ref[tile, n], emf_ref[after, n]) for n in range(3)
-        ]
+        around = [(emf_ref[before, n], emf_ref[tile, n], emf_ref[after, n]) for n in range(3)]
         across_z = plus_y(around[0][1], around[0][2]) - minus_y(around[0][0], around[0][1])
         pair = around[1][1] + minus_y(around[1][0], around[1][1])
         across_x = plus_y(around[2][1], around[2][2]) - minus_y(around[2][0], around[2][1])
@@ -548,8 +559,15 @@
         out_ref[5, rows, columns] = part_ref[tile, 6] - 0.25 * TIME_STEP * pair
         out_ref[6, rows, columns] = part_ref[tile, 7] + 0.25 * TIME_STEP * across_x
 
-    for tile in range(8):
-        last(tile)
+    def step(block):
+        row = pl.multiple_of(block * 8, 8)
+        work_out(row)
+        for tile in range(9):
+            first(row, tile)
+        for tile in range(8):
+            last(row, tile)
+
+    return before_first, step
 
 
 def per_device(state, row_shift, row_frac, edge_shift, edge_frac):
@@ -577,6 +595,7 @@
             vmem(*SLOTS, PIECES, LINES, TILE),
             vmem(GHOSTS * 16, TILE),
             vmem(9, 5, 8, TILE), vmem(9, 8, 8, TILE), vmem(9, 3, 8, TILE),
+            vmem(9, 7, 48, TILE), vmem(8, 5, 48, TILE),
             dma((3,)), dma, dma, dma, dma, dma((PARTS,)), dma, dma((PARTS,)), dma, dma((3,)), dma((3,)),
         ],
         compiler_params=pltpu.CompilerParams(

time: 42.4 us -> 41.9 us (0.988)
  Pallas kernels: 39.9 us -> 39.4 us
    pallas_call x1, Pallas kernels: 39.9 us -> 39.4 us  [per_device(): pl.pallas_call(kernel, out_shape=jax.ShapeDtypeStruct((FIELDS, ROWS, COLU...]
where the time goes in v6:
time: 41.9 us; the launch traced here: 41.7 us
  Pallas kernels  39.4 us (94%)
  between operations  1.3 us (3%)
  local copies, waits for them, and re-layouts  0.97 us (2%)
    pallas_call x1, Pallas kernels, per_device(): pl.pallas_call(kernel, out_shape=jax.ShapeDtypeStruct((FIELDS, ROWS, COLU...  39.4 us
    unnamed x1, local copies, waits for them, and re-layouts  0.97 us

profile of v6, /device:TPU:1, one launch (start us, length us, event | category | flops | bytes accessed | tf_op | source)
XLA Modules:
  0.0 41.7 jit_solution(11570518557612662878)
XLA Ops:
  1.3 39.4 %step.1 = f32[8,32,1024]{2,1,0:T(8,128)S(1)} custom-call(f32[2048,128]{1,0:T(8,128)} %bitcast.5, s32[128]{0:T(128)} %shift_hbm.1, f32[128]{0:T(128)} %frac_hbm.1, s32[1]{0:T(128)S(6)} %copy.7.edge_shift_ref, f32[1]{0:T(128)S(6)} %copy.8.edge_frac_ref), custom_call_target="tpu_custom_call" | custom-call | tf_op jit(solution)/shard_map/step/pallas_call | solution.py:581
  40.7 1.0 %copy.9 = f32[8,32,1024]{2,1,0:T(8,128)} copy(f32[8,32,1024]{2,1,0:T(8,128)S(1)} %step.1) | data formatting | bytes 2097152

commit v7 on v6

--- a/solution.py
+++ b/solution.py
@@ -19,12 +19,19 @@
 TILES = RING * COLUMNS // TILE
 PAD = 24
 WINDOW = 18
+SHORT = 17
 LINES = 24
 SLOTS = (6, 8)
-BX_PIECE = 2
+B_PIECE = 2
 GHOSTS = 17
 VMEM_LIMIT = 28 * 2**20
 TIME_STEP = 0.2
+
+
+def share(lane, v):
+    at = jnp.where(lane < TILE // 2, lane - NZ, lane + NZ)
+    middle = jnp.logical_and(lane >= NZ, lane < TILE - NZ)
+    return jnp.take_along_axis(v, jnp.where(middle, at, lane), axis=1, mode="promise_in_bounds")
 
 
 def place():
@@ -200,6 +207,7 @@
             outer = term if outer is None else outer + term
         return inner, outer
 
+    middle = jnp.logical_and(lane >= NZ, lane < TILE - NZ)
     odd = lax.broadcasted_iota(jnp.int32, (8, TILE), 0) % 2 == 1
 
     def ghost_taps():
@@ -249,21 +257,28 @@
             )
             for f in range(HELD):
                 moved_ref[part, d, f * 8 : f * 8 + 8] = inner[f]
-            moved_ref[part, d, HELD * 8 :] = outer
+            second = share(lane, pltpu.roll(outer, 1, 0))
+            shared = jnp.where(jnp.logical_and(middle, piece != B_PIECE), second, outer)
+            moved_ref[part, d, HELD * 8 :] = shared
 
         def some(j, carry):
             ds = [target(j * GROUPED + m) for m in range(GROUPED)]
             for d in ds:
                 fill(d)
-            for d in ds:
-                pltpu.make_async_remote_copy(
-                    src_ref=moved_ref.at[part, d, :WINDOW],
-                    dst_ref=cells_ref.at[eighth + 1, rest, piece, :WINDOW],
-                    send_sem=back_sem,
-                    recv_sem=row_sem.at[part],
-                    device_id={"az": d, "rad": group},
-                    device_id_type=MESH,
-                ).start()
+
+            def send(size):
+                for d in ds:
+                    pltpu.make_async_remote_copy(
+                        src_ref=moved_ref.at[part, d, :size],
+                        dst_ref=cells_ref.at[eighth + 1, rest, piece, :size],
+                        send_sem=back_sem,
+                        recv_sem=row_sem.at[part],
+                        device_id={"az": d, "rad": group},
+                        device_id_type=MESH,
+                    ).start()
+
+            pl.when(piece == B_PIECE)(lambda: send(WINDOW))
+            pl.when(piece != B_PIECE)(lambda: send(SHORT))
             return carry
 
         lax.fori_loop(0, RING // GROUPED, some, 0)
@@ -302,8 +317,11 @@
         if part == 0:
             pl.when(has_ghost)(send_ghosts)
 
+    lines_ref = cells_ref.reshape(SLOTS[0] * SLOTS[1] * PIECES * LINES, TILE)
+
     def arrived(part):
-        same_size(cells_ref.at[1, :, :, :WINDOW], back_sem, row_sem.at[part]).wait_recv()
+        lines = 8 * (3 * SHORT + WINDOW)
+        same_size(lines_ref.at[:lines], back_sem, row_sem.at[part]).wait_recv()
 
     def hand(source, slot, n, neighbour):
         return pltpu.make_async_remote_copy(
@@ -315,10 +333,16 @@
             device_id_type=MESH,
         )
 
-    to_outer = [hand(cells_ref.at[4, 7, :, :WINDOW], cells_ref.at[0, 7, :, :WINDOW], 0, (rad + 1) % 4)]
+    outer, inner = (rad + 1) % 4, (rad + 3) % 4
+    last = (B_PIECE, slice(SHORT, WINDOW))
+    to_outer = [
+        hand(cells_ref.at[4, 7, :, :SHORT], cells_ref.at[0, 7, :, :SHORT], 0, outer),
+        hand(cells_ref.at[4, 7, *last], cells_ref.at[0, 7, *last], 1, outer),
+    ]
     to_inner = [
-        hand(cells_ref.at[1, 0, :, :WINDOW], cells_ref.at[5, 0, :, :WINDOW], 1, (rad + 3) % 4),
-        hand(cells_ref.at[1, 1, BX_PIECE, :WINDOW], cells_ref.at[5, 1, BX_PIECE, :WINDOW], 2, (rad + 3) % 4),
+        hand(cells_ref.at[1, 0, :, :SHORT], cells_ref.at[5, 0, :, :SHORT], 2, inner),
+        hand(cells_ref.at[1, 0, *last], cells_ref.at[5, 0, *last], 3, inner),
+        hand(cells_ref.at[1, 1, B_PIECE, :SHORT], cells_ref.at[5, 1, B_PIECE, :SHORT], 4, inner),
     ]
     arrived(0)
 
@@ -331,8 +355,6 @@
     def _():
         for copy in to_inner:
             copy.start()
-
-    lines_ref = cells_ref.reshape(SLOTS[0] * SLOTS[1] * PIECES * LINES, TILE)
 
     def take_ghosts(ghosts):
         same_size(ghosts_ref.at[: len(ghosts) * 9], ghosts_back_sem, ghosts_sem).wait_recv()
@@ -341,7 +363,13 @@
             first = ((row + 8) * PIECES + field // HELD) * LINES
             at, ninth = first + field % HELD * 8, first + HELD * 8 + field % HELD
             lines_ref[at : at + 8, :] = ghosts_ref[n * 16 : n * 16 + 8]
-            lines_ref[ninth : ninth + 1, :] = ghosts_ref[n * 16 + 8 : n * 16 + 9]
+            line = ghosts_ref[n * 16 + 8 : n * 16 + 9]
+            if field // HELD == B_PIECE:
+                lines_ref[ninth : ninth + 1, :] = line
+            elif field % HELD == 0:
+                second = jnp.broadcast_to(ghosts_ref[n * 16 + 24 : n * 16 + 25], (8, TILE))
+                both = jnp.where(middle, share(lane, second), jnp.broadcast_to(line, (8, TILE)))
+                lines_ref[ninth : ninth + 1, :] = both[:1]
 
     def received(copies):
         for copy in copies:
@@ -371,7 +399,9 @@
     lax.fori_loop(0, ROWS // 8, one, 0)
 
     same_size(rows_ref, rows_sem, held_sem.at[0]).wait_send()
-    same_size(moved_ref.at[:, :, :WINDOW], back_sem, held_sem.at[0]).wait_send()
+    for size, sent in ((WINDOW, piece == B_PIECE), (SHORT, piece != B_PIECE)):
+        whole = same_size(moved_ref.at[:, :, :size], back_sem, held_sem.at[0])
+        pl.when(sent)(whole.wait_send)
 
     @pl.when(rad == 3)
     def _():
@@ -420,7 +450,7 @@
     left_state = [before[0], *before[1], before[3]]
     right_state = [cell[0], *cell[1], cell[3]]
     return [
-        0.5 * ((left[n] + right[n]) - bound * (right_state[n] - left_state[n])) for n in range(5)
+        (left[n] + right[n]) - bound * (right_state[n] - left_state[n]) for n in range(5)
     ]
 
 
@@ -450,7 +480,17 @@
     def lines_of(row):
         return pl.ds(pl.multiple_of(row + 16, 8), 8)
 
+    def part_lines(row):
+        for piece in range(PIECES):
+            if piece != B_PIECE:
+                first = ((row + 8) * PIECES + piece) * LINES + HELD * 8
+                both = cells_ref[pl.ds(first, 8, stride=PIECES * LINES), :]
+                at = jnp.where(lane < NZ, lane + NZ, jnp.where(lane < TILE - NZ, lane, lane - NZ))
+                second = jnp.take_along_axis(both, at, axis=1, mode="promise_in_bounds")
+                cells_ref[pl.ds(first + 1, 8, stride=PIECES * LINES), :] = second
+
     def work_out(row):
+        part_lines(row + 1)
         for tile in range(9):
             density = load(0, row + 1, tile)
             faces = [load(n, row + 1, tile) for n in (4, 5, 6)]
@@ -536,7 +576,7 @@
         state = [density, *momenta, tracer]
         for n in range(5):
             change = (flux_high[n] - flux_low[n]) + (plus_z(flux_z[n]) - flux_z[n])
-            value = state[n] - TIME_STEP * change
+            value = state[n] - 0.5 * TIME_STEP * change
             if n == 1:
                 value = value + TIME_STEP * 2.0 * momenta[1]
             if n == 2:
@@ -548,7 +588,7 @@
         rows, columns = pl.ds(row, 8), pl.ds(tile * TILE, TILE)
         for n, field in enumerate((0, 1, 2, 3, 7)):
             flux = flux_ref[tile, n]
-            out_ref[field, rows, columns] = part_ref[tile, n] - TIME_STEP * (
+            out_ref[field, rows, columns] = part_ref[tile, n] - 0.5 * TIME_STEP * (
                 plus_y(flux, flux_ref[after, n]) - flux
             )
         around = [(emf_ref[before, n], emf_ref[tile, n], emf_ref[after, n]) for n in range(3)]
@@ -596,7 +636,7 @@
             vmem(GHOSTS * 16, TILE),
             vmem(9, 5, 8, TILE), vmem(9, 8, 8, TILE), vmem(9, 3, 8, TILE),
             vmem(9, 7, 48, TILE), vmem(8, 5, 48, TILE),
-            dma((3,)), dma, dma, dma, dma, dma((PARTS,)), dma, dma((PARTS,)), dma, dma((3,)), dma((3,)),
+            dma((3,)), dma, dma, dma, dma, dma((PARTS,)), dma, dma((PARTS,)), dma, dma((5,)), dma((5,)),
         ],
         compiler_params=pltpu.CompilerParams(
             collective_id=0, has_side_effects=True, vmem_limit_bytes=VMEM_LIMIT

time: 41.9 us -> 41.5 us (level)
  no operation moved by 1% of the time
where the time goes in v7:
time: 41.5 us; the launch traced here: 41.3 us
  Pallas kernels  39 us (94%)
  between operations  1.3 us (3%)
  local copies, waits for them, and re-layouts  0.97 us (2%)
    pallas_call x1, Pallas kernels, per_device(): pl.pallas_call(kernel, out_shape=jax.ShapeDtypeStruct((FIELDS, ROWS, COLU...  39 us
    unnamed x1, local copies, waits for them, and re-layouts  0.97 us

profile of v7, /device:TPU:1, one launch (start us, length us, event | category | flops | bytes accessed | tf_op | source)
XLA Modules:
  0.0 41.3 jit_solution(16935145225480551814)
XLA Ops:
  1.3 39.0 %step.1 = f32[8,32,1024]{2,1,0:T(8,128)S(1)} custom-call(f32[2048,128]{1,0:T(8,128)} %bitcast.5, s32[128]{0:T(128)} %shift_hbm.1, f32[128]{0:T(128)} %frac_hbm.1, s32[1]{0:T(128)S(6)} %copy.7.edge_shift_ref, f32[1]{0:T(128)S(6)} %copy.8.edge_frac_ref), custom_call_target="tpu_custom_call" | custom-call | tf_op jit(solution)/shard_map/step/pallas_call | solution.py:621
  40.4 1.0 %copy.9 = f32[8,32,1024]{2,1,0:T(8,128)} copy(f32[8,32,1024]{2,1,0:T(8,128)S(1)} %step.1) | data formatting | bytes 2097152

commit v8 on v7

--- a/solution.py
+++ b/solution.py
@@ -21,6 +21,7 @@
 WINDOW = 18
 SHORT = 17
 LINES = 24
+ROW_LINES = 104
 SLOTS = (6, 8)
 B_PIECE = 2
 GHOSTS = 17
@@ -270,7 +271,7 @@
                 for d in ds:
                     pltpu.make_async_remote_copy(
                         src_ref=moved_ref.at[part, d, :size],
-                        dst_ref=cells_ref.at[eighth + 1, rest, piece, :size],
+                        dst_ref=cells_ref.at[eighth + 1, rest, pl.ds(piece * LINES, size)],
                         send_sem=back_sem,
                         recv_sem=row_sem.at[part],
                         device_id={"az": d, "rad": group},
@@ -317,7 +318,7 @@
         if part == 0:
             pl.when(has_ghost)(send_ghosts)
 
-    lines_ref = cells_ref.reshape(SLOTS[0] * SLOTS[1] * PIECES * LINES, TILE)
+    lines_ref = cells_ref.reshape(SLOTS[0] * SLOTS[1] * ROW_LINES, TILE)
 
     def arrived(part):
         lines = 8 * (3 * SHORT + WINDOW)
@@ -334,16 +335,19 @@
         )
 
     outer, inner = (rad + 1) % 4, (rad + 3) % 4
-    last = (B_PIECE, slice(SHORT, WINDOW))
+    windows = [
+        pl.ds(n * LINES, WINDOW if n == B_PIECE else SHORT) for n in range(PIECES)
+    ]
     to_outer = [
-        hand(cells_ref.at[4, 7, :, :SHORT], cells_ref.at[0, 7, :, :SHORT], 0, outer),
-        hand(cells_ref.at[4, 7, *last], cells_ref.at[0, 7, *last], 1, outer),
+        hand(cells_ref.at[4, 7, window], cells_ref.at[0, 7, window], n, outer)
+        for n, window in enumerate(windows)
     ]
     to_inner = [
-        hand(cells_ref.at[1, 0, :, :SHORT], cells_ref.at[5, 0, :, :SHORT], 2, inner),
-        hand(cells_ref.at[1, 0, *last], cells_ref.at[5, 0, *last], 3, inner),
-        hand(cells_ref.at[1, 1, B_PIECE, :SHORT], cells_ref.at[5, 1, B_PIECE, :SHORT], 4, inner),
+        hand(cells_ref.at[1, 0, window], cells_ref.at[5, 0, window], PIECES + n, inner)
+        for n, window in enumerate(windows)
     ]
+    faces = pl.ds(B_PIECE * LINES, SHORT)
+    to_inner.append(hand(cells_ref.at[1, 1, faces], cells_ref.at[5, 1, faces], 2 * PIECES, inner))
     arrived(0)
 
     @pl.when(rad < 3)
@@ -360,7 +364,7 @@
         same_size(ghosts_ref.at[: len(ghosts) * 9], ghosts_back_sem, ghosts_sem).wait_recv()
         for n in ghosts:
             row, field = (-1, n) if n < 8 else (ROWS, n - 8) if n < 16 else (ROWS + 1, 4)
-            first = ((row + 8) * PIECES + field // HELD) * LINES
+            first = (row + 8) * ROW_LINES + field // HELD * LINES
             at, ninth = first + field % HELD * 8, first + HELD * 8 + field % HELD
             lines_ref[at : at + 8, :] = ghosts_ref[n * 16 : n * 16 + 8]
             line = ghosts_ref[n * 16 + 8 : n * 16 + 9]
@@ -462,8 +466,8 @@
 
     def load(field, row, tile):
         line = field % HELD * 8 + tile if tile < 8 else HELD * 8 + field % HELD
-        first = ((row + 8) * PIECES + field // HELD) * LINES + line
-        return cells_ref[pl.ds(first, 8, stride=PIECES * LINES), :]
+        first = (row + 8) * ROW_LINES + field // HELD * LINES + line
+        return cells_ref[pl.ds(first, 8, stride=ROW_LINES), :]
 
     def plus_z(v):
         return jnp.take_along_axis(v, up, axis=1, mode="promise_in_bounds")
@@ -483,11 +487,11 @@
     def part_lines(row):
         for piece in range(PIECES):
             if piece != B_PIECE:
-                first = ((row + 8) * PIECES + piece) * LINES + HELD * 8
-                both = cells_ref[pl.ds(first, 8, stride=PIECES * LINES), :]
+                first = (row + 8) * ROW_LINES + piece * LINES + HELD * 8
+                both = cells_ref[pl.ds(first, 8, stride=ROW_LINES), :]
                 at = jnp.where(lane < NZ, lane + NZ, jnp.where(lane < TILE - NZ, lane, lane - NZ))
                 second = jnp.take_along_axis(both, at, axis=1, mode="promise_in_bounds")
-                cells_ref[pl.ds(first + 1, 8, stride=PIECES * LINES), :] = second
+                cells_ref[pl.ds(first + 1, 8, stride=ROW_LINES), :] = second
 
     def work_out(row):
         part_lines(row + 1)
@@ -632,11 +636,11 @@
             vmem(TILES + PAD, TILE),
             vmem(PARTS, RING, LINES, TILE),
             vmem(RING, 16, TILE),
-            vmem(*SLOTS, PIECES, LINES, TILE),
+            vmem(*SLOTS, ROW_LINES, TILE),
             vmem(GHOSTS * 16, TILE),
             vmem(9, 5, 8, TILE), vmem(9, 8, 8, TILE), vmem(9, 3, 8, TILE),
             vmem(9, 7, 48, TILE), vmem(8, 5, 48, TILE),
-            dma((3,)), dma, dma, dma, dma, dma((PARTS,)), dma, dma((PARTS,)), dma, dma((5,)), dma((5,)),
+            dma((3,)), dma, dma, dma, dma, dma((PARTS,)), dma, dma((PARTS,)), dma, dma((9,)), dma((9,)),
         ],
         compiler_params=pltpu.CompilerParams(
             collective_id=0, has_side_effects=True, vmem_limit_bytes=VMEM_LIMIT

time: 41.5 us -> 41.2 us (level)
  no operation moved by 1% of the time
where the time goes in v8:
time: 41.2 us; the launch traced here: 41.1 us
  Pallas kernels  38.8 us (94%)
  between operations  1.3 us (3%)
  local copies, waits for them, and re-layouts  0.97 us (2%)
    pallas_call x1, Pallas kernels, per_device(): pl.pallas_call(kernel, out_shape=jax.ShapeDtypeStruct((FIELDS, ROWS, COLU...  38.8 us
    unnamed x1, local copies, waits for them, and re-layouts  0.97 us

profile of v8, /device:TPU:1, one launch (start us, length us, event | category | flops | bytes accessed | tf_op | source)
XLA Modules:
  0.0 41.1 jit_solution(12415605644280515398)
XLA Ops:
  1.3 38.8 %step.1 = f32[8,32,1024]{2,1,0:T(8,128)S(1)} custom-call(f32[2048,128]{1,0:T(8,128)} %bitcast.5, s32[128]{0:T(128)} %shift_hbm.1, f32[128]{0:T(128)} %frac_hbm.1, s32[1]{0:T(128)S(6)} %copy.7.edge_shift_ref, f32[1]{0:T(128)S(6)} %copy.8.edge_frac_ref), custom_call_target="tpu_custom_call" | custom-call | tf_op jit(solution)/shard_map/step/pallas_call | solution.py:625
  40.1 1.0 %copy.9 = f32[8,32,1024]{2,1,0:T(8,128)} copy(f32[8,32,1024]{2,1,0:T(8,128)S(1)} %step.1) | data formatting | bytes 2097152

commit v9 on v8

--- a/solution.py
+++ b/solution.py
@@ -606,10 +606,12 @@
     def step(block):
         row = pl.multiple_of(block * 8, 8)
         work_out(row)
-        for tile in range(9):
+        first(row, 8)
+        first(row, 0)
+        for tile in range(1, 8):
             first(row, tile)
-        for tile in range(8):
-            last(row, tile)
+            last(row, tile - 1)
+        last(row, 7)
 
     return before_first, step
 

time: 41.2 us -> 41.1 us (level)
  no operation moved by 1% of the time
where the time goes in v9:
time: 41.1 us; the launch traced here: 40.9 us
  Pallas kernels  38.7 us (94%)
  between operations  1.3 us (3%)
  local copies, waits for them, and re-layouts  0.97 us (2%)
    pallas_call x1, Pallas kernels, per_device(): pl.pallas_call(kernel, out_shape=jax.ShapeDtypeStruct((FIELDS, ROWS, COLU...  38.7 us
    unnamed x1, local copies, waits for them, and re-layouts  0.97 us

profile of v9, /device:TPU:1, one launch (start us, length us, event | category | flops | bytes accessed | tf_op | source)
XLA Modules:
  0.0 40.9 jit_solution(13542293541563745706)
XLA Ops:
  1.3 38.7 %step.1 = f32[8,32,1024]{2,1,0:T(8,128)S(1)} custom-call(f32[2048,128]{1,0:T(8,128)} %bitcast.5, s32[128]{0:T(128)} %shift_hbm.1, f32[128]{0:T(128)} %frac_hbm.1, s32[1]{0:T(128)S(6)} %copy.7.edge_shift_ref, f32[1]{0:T(128)S(6)} %copy.8.edge_frac_ref), custom_call_target="tpu_custom_call" | custom-call | tf_op jit(solution)/shard_map/step/pallas_call | solution.py:627
  40.0 1.0 %copy.9 = f32[8,32,1024]{2,1,0:T(8,128)} copy(f32[8,32,1024]{2,1,0:T(8,128)S(1)} %step.1) | data formatting | bytes 2097152

commit v10 on v9

--- a/solution.py
+++ b/solution.py
@@ -21,7 +21,7 @@
 WINDOW = 18
 SHORT = 17
 LINES = 24
-ROW_LINES = 104
+ROW_LINES = 100
 SLOTS = (6, 8)
 B_PIECE = 2
 GHOSTS = 17
@@ -209,6 +209,11 @@
         return inner, outer
 
     middle = jnp.logical_and(lane >= NZ, lane < TILE - NZ)
+    lines_ref = cells_ref
+
+    def lines_at(slot, n, size):
+        return pl.ds(slot * ROW_LINES + n * LINES, size)
+
     odd = lax.broadcasted_iota(jnp.int32, (8, TILE), 0) % 2 == 1
 
     def ghost_taps():
@@ -271,7 +276,7 @@
                 for d in ds:
                     pltpu.make_async_remote_copy(
                         src_ref=moved_ref.at[part, d, :size],
-                        dst_ref=cells_ref.at[eighth + 1, rest, pl.ds(piece * LINES, size)],
+                        dst_ref=lines_ref.at[lines_at((eighth + 1) * 8 + rest, piece, size)],
                         send_sem=back_sem,
                         recv_sem=row_sem.at[part],
                         device_id={"az": d, "rad": group},
@@ -318,8 +323,6 @@
         if part == 0:
             pl.when(has_ghost)(send_ghosts)
 
-    lines_ref = cells_ref.reshape(SLOTS[0] * SLOTS[1] * ROW_LINES, TILE)
-
     def arrived(part):
         lines = 8 * (3 * SHORT + WINDOW)
         same_size(lines_ref.at[:lines], back_sem, row_sem.at[part]).wait_recv()
@@ -335,19 +338,22 @@
         )
 
     outer, inner = (rad + 1) % 4, (rad + 3) % 4
-    windows = [
-        pl.ds(n * LINES, WINDOW if n == B_PIECE else SHORT) for n in range(PIECES)
-    ]
-    to_outer = [
-        hand(cells_ref.at[4, 7, window], cells_ref.at[0, 7, window], n, outer)
-        for n, window in enumerate(windows)
-    ]
-    to_inner = [
-        hand(cells_ref.at[1, 0, window], cells_ref.at[5, 0, window], PIECES + n, inner)
-        for n, window in enumerate(windows)
-    ]
-    faces = pl.ds(B_PIECE * LINES, SHORT)
-    to_inner.append(hand(cells_ref.at[1, 1, faces], cells_ref.at[5, 1, faces], 2 * PIECES, inner))
+    sizes = [WINDOW if n == B_PIECE else SHORT for n in range(PIECES)]
+
+    def hand_row(source, slot, pieces, first, neighbour):
+        return [
+            hand(
+                lines_ref.at[lines_at(source, n, sizes[n])],
+                lines_ref.at[lines_at(slot, n, sizes[n])],
+                first + n,
+                neighbour,
+            )
+            for n in pieces
+        ]
+
+    to_outer = hand_row(39, 7, range(PIECES), 0, outer)
+    to_inner = hand_row(8, 40, range(PIECES), PIECES, inner)
+    to_inner += hand_row(9, 41, (B_PIECE,), 2 * PIECES - B_PIECE, inner)
     arrived(0)
 
     @pl.when(rad < 3)
@@ -638,7 +644,7 @@
             vmem(TILES + PAD, TILE),
             vmem(PARTS, RING, LINES, TILE),
             vmem(RING, 16, TILE),
-            vmem(*SLOTS, ROW_LINES, TILE),
+            vmem(SLOTS[0] * SLOTS[1] * ROW_LINES, TILE),
             vmem(GHOSTS * 16, TILE),
             vmem(9, 5, 8, TILE), vmem(9, 8, 8, TILE), vmem(9, 3, 8, TILE),
             vmem(9, 7, 48, TILE), vmem(8, 5, 48, TILE),

time: 41.1 us -> 41.1 us (level)
  no operation moved by 1% of the time
where the time goes in v10:
time: 41.1 us; the launch traced here: 40.9 us
  Pallas kernels  38.6 us (94%)
  between operations  1.3 us (3%)
  local copies, waits for them, and re-layouts  0.97 us (2%)
    pallas_call x1, Pallas kernels, per_device(): pl.pallas_call(kernel, out_shape=jax.ShapeDtypeStruct((FIELDS, ROWS, COLU...  38.6 us
    unnamed x1, local copies, waits for them, and re-layouts  0.97 us

profile of v10, /device:TPU:1, one launch (start us, length us, event | category | flops | bytes accessed | tf_op | source)
XLA Modules:
  0.0 40.9 jit_solution(16266991635424292691)
XLA Ops:
  1.3 38.6 %step.1 = f32[8,32,1024]{2,1,0:T(8,128)S(1)} custom-call(f32[2048,128]{1,0:T(8,128)} %bitcast.5, s32[128]{0:T(128)} %shift_hbm.1, f32[128]{0:T(128)} %frac_hbm.1, s32[1]{0:T(128)S(6)} %copy.7.edge_shift_ref, f32[1]{0:T(128)S(6)} %copy.8.edge_frac_ref), custom_call_target="tpu_custom_call" | custom-call | tf_op jit(solution)/shard_map/step/pallas_call | solution.py:633
  40.0 1.0 %copy.9 = f32[8,32,1024]{2,1,0:T(8,128)} copy(f32[8,32,1024]{2,1,0:T(8,128)S(1)} %step.1) | data formatting | bytes 2097152

commit v11 on v10

--- a/solution.py
+++ b/solution.py
@@ -575,12 +575,13 @@
 
         flux_high = outer_flux(row, tile, cell)
         flux_low = [side_ref[tile, n, pl.ds(row + 15, 8), :] for n in range(5)]
+        below_density = minus_z(density)
         below = (
-            minus_z(density),
+            below_density,
             [minus_z(m) for m in momenta],
             [minus_z(centred[0]), minus_z(centred[1]), None],
             minus_z(tracer),
-            minus_z(inverse),
+            1.0 / below_density,
         )
         flux_z = face_flux(below, cell, 2, faces[2])
         state = [density, *momenta, tracer]

time: 41.1 us -> 41.1 us (level)
  no operation moved by 1% of the time
where the time goes in v11:
time: 41.1 us; the launch traced here: 40.9 us
  Pallas kernels  38.6 us (94%)
  between operations  1.3 us (3%)
  local copies, waits for them, and re-layouts  0.97 us (2%)
    pallas_call x1, Pallas kernels, per_device(): pl.pallas_call(kernel, out_shape=jax.ShapeDtypeStruct((FIELDS, ROWS, COLU...  38.6 us
    unnamed x1, local copies, waits for them, and re-layouts  0.97 us

profile of v11, /device:TPU:1, one launch (start us, length us, event | category | flops | bytes accessed | tf_op | source)
XLA Modules:
  0.0 40.9 jit_solution(12007322626433622251)
XLA Ops:
  1.3 38.6 %step.1 = f32[8,32,1024]{2,1,0:T(8,128)S(1)} custom-call(f32[2048,128]{1,0:T(8,128)} %bitcast.5, s32[128]{0:T(128)} %shift_hbm.1, f32[128]{0:T(128)} %frac_hbm.1, s32[1]{0:T(128)S(6)} %copy.7.edge_shift_ref, f32[1]{0:T(128)S(6)} %copy.8.edge_frac_ref), custom_call_target="tpu_custom_call" | custom-call | tf_op jit(solution)/shard_map/step/pallas_call | solution.py:634
  39.9 1.0 %copy.9 = f32[8,32,1024]{2,1,0:T(8,128)} copy(f32[8,32,1024]{2,1,0:T(8,128)S(1)} %step.1) | data formatting | bytes 2097152

commit v12 on v10

--- a/solution.py
+++ b/solution.py
@@ -390,10 +390,10 @@
     def one(block, carry):
         @pl.when(block == 0)
         def _():
-            arrived(1)
             pl.when(rad > 0)(lambda: received(to_outer))
             pl.when(rad == 0)(lambda: take_ghosts(range(8)))
             before_first()
+            arrived(1)
 
         pl.when(block == 1)(lambda: arrived(2))
 

time: 41.1 us -> 41.1 us (level)
  no operation moved by 1% of the time
where the time goes in v12:
time: 41.1 us; the launch traced here: 40.9 us
  Pallas kernels  38.6 us (94%)
  between operations  1.3 us (3%)
  local copies, waits for them, and re-layouts  0.97 us (2%)
    pallas_call x1, Pallas kernels, per_device(): pl.pallas_call(kernel, out_shape=jax.ShapeDtypeStruct((FIELDS, ROWS, COLU...  38.6 us
    unnamed x1, local copies, waits for them, and re-layouts  0.97 us

profile of v12, /device:TPU:1, one launch (start us, length us, event | category | flops | bytes accessed | tf_op | source)
XLA Modules:
  0.0 40.9 jit_solution(17779653272021916726)
XLA Ops:
  1.3 38.6 %step.1 = f32[8,32,1024]{2,1,0:T(8,128)S(1)} custom-call(f32[2048,128]{1,0:T(8,128)} %bitcast.5, s32[128]{0:T(128)} %shift_hbm.1, f32[128]{0:T(128)} %frac_hbm.1, s32[1]{0:T(128)S(6)} %copy.7.edge_shift_ref, f32[1]{0:T(128)S(6)} %copy.8.edge_frac_ref), custom_call_target="tpu_custom_call" | custom-call | tf_op jit(solution)/shard_map/step/pallas_call | solution.py:633
  40.0 1.0 %copy.9 = f32[8,32,1024]{2,1,0:T(8,128)} copy(f32[8,32,1024]{2,1,0:T(8,128)S(1)} %step.1) | data formatting | bytes 2097152
